TPU v7x, 512 devices: a whole 4x8x8 slice. The times are simulated.
512 devices in a mesh: dp: 8 (over z), fsdp: 8 (over x, core), tensor: 8 (over y).
Axes of the slice: x: 4, y: 8, z: 8, core: 2. Of those that a mesh axis runs over, the one named last changes fastest.
Arguments:
- momentum: float32 [8, 1, 7168, 2048], P('dp', None, 'fsdp', 'tensor'), may hold values from -500 to 500
- gradient: bfloat16 [8, 1, 7168, 2048], P('dp', None, 'fsdp', 'tensor'), may hold values from -3 to 3
- right_factor: float32 [1, 2048, 128], P(None, 'tensor'), may hold values from -0.125 to 0.125
Outputs:
- new_momentum: float32 [8, 1, 7168, 2048], P('dp', None, 'fsdp', 'tensor')
- right_out: float32 [1, 2048, 128], P(None, 'tensor')
- update: bfloat16 [1, 7168, 2048], P(None, 'fsdp', 'tensor')
All inputs are finite; a program needn't handle non-finite values.
Results may differ from a plain program's by a relative error of at most 0.001.
Values sent between devices are 32-bit elements; how exact they have to be, the bound alone decides.
No kernel may reach another device: no remote copies, remote signals or barrier semaphores. Data moves between devices by JAX's collectives and lax.ppermute only.
A program may use at most 64 MiB of HBM per device.

v0:
```python
import math

import jax
import jax.numpy as jnp
from jax import lax
from jax.sharding import PartitionSpec as P

M_ROWS = 7168
N_COLS = 2048
RANK = 128


highest = lax.Precision.HIGHEST
decay_rate = 0.95
epsilon = 1e-06


def product(left, right):
    return jnp.dot(left, right, precision=highest, preferred_element_type=jnp.float32)


def inner_rows(left, right):
    return lax.dot_general(
        left, right, (((0,), (0,)), ((), ())), precision=highest, preferred_element_type=jnp.float32
    )


def outer_cols(left, right):
    return lax.dot_general(
        left, right, (((1,), (1,)), ((), ())), precision=highest, preferred_element_type=jnp.float32
    )


def whiten(matrix, factor_low):
    return jax.scipy.linalg.solve_triangular(factor_low, matrix.T, lower=True).T


def body(momentum, gradient, right_factor):
    replicas = lax.axis_size("dp")
    blended = momentum[0, 0] + gradient[0, 0].astype(jnp.float32)
    right_local = right_factor[0]
    projected = lax.psum(product(blended, right_local), ("dp", "tensor"))
    factor_low = jnp.linalg.cholesky(lax.psum(inner_rows(projected, projected), "fsdp"))
    projected = whiten(projected, factor_low)
    reduced = lax.psum(inner_rows(blended, projected), ("dp", "fsdp"))
    reduced = reduced / replicas
    squares = lax.psum(jnp.sum(reduced * reduced, axis=0), "tensor")
    right_new = reduced / (jnp.sqrt(squares) + epsilon)
    moments = [blended - (1.0 - decay_rate) * outer_cols(projected, reduced)]
    rights = [right_new]
    direction = outer_cols(projected, right_new)
    updates = [(math.sqrt(M_ROWS * N_COLS / RANK) * direction).astype(jnp.bfloat16)]
    return (jnp.stack(moments)[None], jnp.stack(rights), jnp.stack(updates))


def solution(mesh):
    in_specs = (
        P("dp", None, "fsdp", "tensor"),
        P("dp", None, "fsdp", "tensor"),
        P(None, "tensor", None),
    )
    out_specs = (
        P("dp", None, "fsdp", "tensor"),
        P(None, "tensor", None),
        P(None, "fsdp", "tensor"),
    )
    return jax.shard_map(body, mesh=mesh, in_specs=in_specs, out_specs=out_specs, check_vma=False)
```

profile of v0, /device:TPU:1, one launch (start us, length us, event | category | flops | bytes accessed | tf_op | source)
XLA Modules:
  0.0 479.4 jit_solution(15603696229998436925)
XLA Ops:
  7.2 0.0 copy-start
  7.2 0.0 all-reduce.4.cloned.1.call-start
  7.2 0.8 copy-done
  8.1 2.9 fusion.6
  11.0 0.0 all-reduce.4.cloned.1.call-update
  11.0 0.0 all-reduce.6.cloned.1.call-start
  11.1 158.3 %all-reduce.4.cloned.1.call-done = f32[896,128]{1,0:T(8,128)} async-done(((f32[896,128]{1,0:T(8,128)}), f32[896,128]{1,0:T(8,128)}) %all-reduce.4.cloned.1.call-update) | async-done | bytes 458768 | tf_op jit(solution)/shard_map/psum | solution.py:42
  169.4 0.0 copy-start.2
  169.4 2.7 fusion.18
  172.1 0.0 copy-start.1
  172.1 0.0 all-reduce.6.cloned.1.call-update
  172.1 0.0 all-reduce.8.cloned.1.call-start
  172.2 68.6 %all-reduce.6.cloned.1.call-done = f32[128,128]{0,1:T(8,128)} async-done(((f32[128,128]{0,1:T(8,128)}), f32[128,128]{0,1:T(8,128)}) %all-reduce.6.cloned.1.call-update) | async-done | bytes 65552 | tf_op jit(solution)/shard_map/psum | solution.py:43
  240.8 0.9 copy.7
  241.8 0.9 fusion.13
  242.6 11.7 %cholesky.16 = f32[128,128]{1,0:T(8,128)S(1)} custom-call(f32[128,128]{1,0:T(8,128)S(1)} %fusion.13), custom_call_target="Cholesky" | custom-call | tf_op jit(solution)/shard_map/jit(cholesky)/cholesky | solution.py:43
  254.4 0.6 compare_reduce_fusion
  255.0 0.7 fusion.10
  255.7 9.8 %custom-call.7 = f32[1,128,128]{1,2,0:T(8,128)S(1)} custom-call(f32[1,128,128]{2,1,0:T(8,128)S(1)} %fusion.10), custom_call_target="InvertDiagBlocksLowerTriangular" | custom-call | tf_op jit(solution)/shard_map/jit(_solve_triangular)/triangular_solve | solution.py:35
  265.5 0.0 copy-done.2
  265.5 0.0 copy-start.3
  265.5 0.6 fusion.11
  266.1 0.0 copy-done.1
  266.1 0.4 copy-done.3
  266.5 2.3 fusion.4
  268.8 0.0 all-reduce.8.cloned.1.call-update
  268.8 185.6 %all-reduce.8.cloned.1.call-done = f32[256,128]{1,0:T(8,128)} async-done(((f32[256,128]{1,0:T(8,128)}), f32[256,128]{1,0:T(8,128)}) %all-reduce.8.cloned.1.call-update) | async-done | bytes 131088 | tf_op jit(solution)/shard_map/psum | solution.py:45
  454.4 0.0 copy-start.4
  454.5 1.0 multiply_reduce_fusion
  455.5 13.2 %psum.31 = f32[128]{0:T(128)S(1)} all-reduce(f32[128]{0:T(128)S(1)} %multiply_reduce_fusion), channel_id=1, replica_groups=mesh['dp'=8,'fsdp'=8,'tensor'=8] {'tensor'}, use_global_device_ids=true, to_apply=%region_6.7 | all-reduce | flops 128 | bytes 1024 | tf_op jit(solution)/shard_map/psum | solution.py:47
  468.7 0.0 copy-done.4
  468.7 0.7 fusion.15
  469.4 1.7 fusion.3
  471.1 1.8 fusion.1
  (2 shorter events, 0.0 us)
Async XLA Ops:
  7.2 0.9 copy-start
  7.2 162.2 %all-reduce.4.cloned.1.call-start = ((), (), s32[]{:S(2)}) async-start(), calls=%async_computation | async-start | bytes 917504 | tf_op jit(solution)/shard_map/psum | solution.py:42
  11.0 229.8 %all-reduce.6.cloned.1.call-start = ((), (), s32[]{:S(2)}) async-start(), calls=%async_computation.1 | async-start | bytes 131072 | tf_op jit(solution)/shard_map/psum | solution.py:43
  169.4 96.1 %copy-start.2 = (f32[896,128]{1,0:T(8,128)S(1)}, f32[896,128]{1,0:T(8,128)}, u32[]{:S(2)}) copy-start(f32[896,128]{1,0:T(8,128)} %all-reduce.4.cloned.1.call-done) | copy-start | bytes 1376260
  172.1 94.0 %copy-start.1 = (f32[1,1,896,256]{3,2,1,0:T(8,128)S(1)}, f32[1,1,896,256]{3,2,1,0:T(8,128)}, u32[]{:S(2)}) copy-start(f32[1,1,896,256]{3,2,1,0:T(8,128)} %param.3) | copy-start | bytes 2752516
  172.1 282.3 %all-reduce.8.cloned.1.call-start = ((), (), s32[]{:S(2)}) async-start(), calls=%async_computation.2 | async-start | bytes 262144 | tf_op jit(solution)/shard_map/psum | solution.py:45
  265.5 1.0 copy-start.3
  454.4 14.3 %copy-start.4 = (f32[256,128]{1,0:T(8,128)S(1)}, f32[256,128]{1,0:T(8,128)}, u32[]{:S(2)}) copy-start(f32[256,128]{1,0:T(8,128)} %all-reduce.8.cloned.1.call-done) | copy-start | bytes 393220
Sparse Core Ops, SparseCore 0:
  11.8 157.4 all-reduce.3
  172.4 68.4 all-reduce.5
  269.0 185.4 all-reduce.7
where the time goes:
time: 481 us; the launch traced here: 479 us
  waiting for transfers between devices  413 us (86%)
  other arithmetic  25.4 us (5%)
  between operations  13.8 us (3%)
  blocking collectives  13.2 us (3%)
  matrix products  12.1 us (3%)
    psum x1, waiting for transfers between devices, body(): reduced = lax.psum(inner_rows(blended, projected), ('dp', 'fsdp'))  186 us
    psum x1, waiting for transfers between devices, body(): projected = lax.psum(product(blended, right_local), ('dp', 'tensor'))  158 us
    psum x1, waiting for transfers between devices, body(): lax.psum(inner_rows(projected, projected), 'fsdp')  68.6 us
    psum x1, blocking collectives, body(): squares = lax.psum(jnp.sum(reduced * reduced, axis=0), 'tensor')  13.2 us
    another operation x3, other arithmetic, body(): jnp.linalg.cholesky(lax.psum(inner_rows(projected, projected), 'fsdp'))  12.4 us
    another operation x2, other arithmetic, whiten(): return jax.scipy.linalg.solve_triangular(factor_low, matrix.T, lower=True).T  10.5 us
  transfers between devices with their start and end apart: 3, of which 3 were waited for; matrix products, arithmetic and copies ran while one was open for 0% of the time, Pallas kernels for 0%

commit v1 on v0

--- a/solution.py
+++ b/solution.py
@@ -35,22 +35,39 @@
     return jax.scipy.linalg.solve_triangular(factor_low, matrix.T, lower=True).T
 
 
+def scatter_sum(blocks, axes):
+    return jnp.sum(lax.all_to_all(blocks, axes, 0, 0), axis=0)
+
+
+def gather(block, axes, count):
+    return lax.all_to_all(jnp.broadcast_to(block, (count,) + block.shape), axes, 0, 0)
+
+
 def body(momentum, gradient, right_factor):
-    replicas = lax.axis_size("dp")
+    n_dp, n_fsdp, n_tensor = (lax.axis_size(a) for a in ("dp", "fsdp", "tensor"))
     blended = momentum[0, 0] + gradient[0, 0].astype(jnp.float32)
-    right_local = right_factor[0]
-    projected = lax.psum(product(blended, right_local), ("dp", "tensor"))
-    factor_low = jnp.linalg.cholesky(lax.psum(inner_rows(projected, projected), "fsdp"))
-    projected = whiten(projected, factor_low)
-    reduced = lax.psum(inner_rows(blended, projected), ("dp", "fsdp"))
-    reduced = reduced / replicas
-    squares = lax.psum(jnp.sum(reduced * reduced, axis=0), "tensor")
+    rows, cols = blended.shape
+    plane = n_dp * n_tensor
+    partial = product(blended, right_factor[0])
+    part = scatter_sum(partial.reshape(plane, rows // plane, RANK), ("dp", "tensor"))
+    projected = gather(part, ("dp", "tensor"), plane).reshape(rows, RANK)
+    right_raw = inner_rows(blended, projected).reshape(n_fsdp, cols // n_fsdp, RANK)
+    gram = inner_rows(projected, projected).reshape(n_fsdp, RANK // n_fsdp, RANK)
+    held = scatter_sum(jnp.concatenate([right_raw, gram], axis=1), "fsdp")
+    own = cols // n_fsdp
+    summed = jnp.sum(gather(held[:own], "dp", n_dp), axis=0)
+    whole = gather(jnp.concatenate([summed, held[own:]], axis=0), "fsdp", n_fsdp)
+    right_raw = whole[:, :own].reshape(cols, RANK)
+    factor_low = jnp.linalg.cholesky(whole[:, own:].reshape(RANK, RANK))
+    both = whiten(jnp.concatenate([projected, right_raw / n_dp], axis=0), factor_low)
+    projected, reduced = both[:rows], both[rows:]
+    squares = jnp.sum(reduced * reduced, axis=0, keepdims=True)
+    squares = jnp.sum(gather(squares, "tensor", n_tensor), axis=0)
     right_new = reduced / (jnp.sqrt(squares) + epsilon)
-    moments = [blended - (1.0 - decay_rate) * outer_cols(projected, reduced)]
-    rights = [right_new]
+    moment = blended - (1.0 - decay_rate) * outer_cols(projected, reduced)
     direction = outer_cols(projected, right_new)
-    updates = [(math.sqrt(M_ROWS * N_COLS / RANK) * direction).astype(jnp.bfloat16)]
-    return (jnp.stack(moments)[None], jnp.stack(rights), jnp.stack(updates))
+    update = (math.sqrt(M_ROWS * N_COLS / RANK) * direction).astype(jnp.bfloat16)
+    return moment[None, None], right_new[None], update[None]
 
 
 def solution(mesh):

time: 481 us -> 139 us (0.29)
  waiting for transfers between devices: 413 us -> 28 us
  blocking collectives: 13.2 us -> 59.5 us
  starting transfers between devices: 0.12 us -> 13.4 us
  between operations: 13.8 us -> 0.85 us
    psum x3 -> x0, waiting for transfers between devices: 413 us -> none  [the longest x1 186 us: body(): reduced = lax.psum(inner_rows(blended, projected), ('dp', 'fsdp'))]
    all_to_all x0 -> x3, blocking collectives: none -> 59.5 us  [the longest x2 48.8 us: scatter_sum(): return jnp.sum(lax.all_to_all(blocks, axes, 0, 0), axis=0)]
    all_to_all x0 -> x3, waiting for transfers between devices: none -> 28 us  [gather(): lax.all_to_all(jnp.broadcast_to(block, (count,) + block.shape), axes, 0, 0)]
    all_to_all x0 -> x3, starting transfers between devices: none -> 13.4 us  [gather(): lax.all_to_all(jnp.broadcast_to(block, (count,) + block.shape), axes, 0, 0)]
    psum x1 -> x0, blocking collectives: 13.2 us -> none  [body(): squares = lax.psum(jnp.sum(reduced * reduced, axis=0), 'tensor')]
    another operation x4 -> x3, other arithmetic: 13.1 us -> 12.4 us  [body(): factor_low = jnp.linalg.cholesky(whole[:, own:].reshape(RANK, RANK))]
  transfers between devices with their start and end apart: 3 -> 3, of which waited for: 3 -> 3; matrix products, arithmetic and copies ran while one was open for 0% -> 2% of each run, Pallas kernels for 0% -> 0%
where the time goes in v1:
time: 139 us
  blocking collectives  59.5 us (43%)
  waiting for transfers between devices  28 us (20%)
  other arithmetic  25.2 us (18%)
  starting transfers between devices  13.4 us (10%)
  matrix products  7.91 us (6%)
  local copies, waits for them, and re-layouts  3.95 us (3%)
    all_to_all x2, blocking collectives, scatter_sum(): return jnp.sum(lax.all_to_all(blocks, axes, 0, 0), axis=0)  48.8 us
    all_to_all x3, waiting for transfers between devices, gather(): lax.all_to_all(jnp.broadcast_to(block, (count,) + block.shape), axes, 0, 0)  28 us
    all_to_all x3, starting transfers between devices, gather(): lax.all_to_all(jnp.broadcast_to(block, (count,) + block.shape), axes, 0, 0)  13.4 us
    another operation x3, other arithmetic, body(): factor_low = jnp.linalg.cholesky(whole[:, own:].reshape(RANK, RANK))  12.4 us
    all_to_all x1, blocking collectives, gather(): lax.all_to_all(jnp.broadcast_to(block, (count,) + block.shape), axes, 0, 0)  10.7 us
    another operation x2, other arithmetic, whiten(): return jax.scipy.linalg.solve_triangular(factor_low, matrix.T, lower=True).T  10.5 us
    dot_general x2, matrix products, outer_cols(): lax.dot_general(left, right, (((1,), (1,)), ((), ())), precision=highest,...  3.48 us
  transfers between devices with their start and end apart: 3, of which 3 were waited for; matrix products, arithmetic and copies ran while one was open for 2% of the time, Pallas kernels for 0%

profile of v1, /device:TPU:1, one launch (start us, length us, event | category | flops | bytes accessed | tf_op | source)
XLA Modules:
  0.0 138.7 jit_solution(15466925200498327908)
XLA Ops:
  0.6 0.0 copy-start
  0.6 1.4 %convert_add_fusion = f32[1,1,896,256]{3,2,1,0:T(8,128)S(1)} fusion(f32[1,1,896,256]{3,2,1,0:T(8,128)} %param.3, bf16[1,1,896,256]{3,2,1,0:T(8,128)(2,1)} %param.4), kind=kLoop, calls=%fused_computation.8 | loop fusion | flops 458752 | bytes 2293760 | tf_op jit(solution)/shard_map/add | solution.py:48
  2.1 0.1 add.35
  2.2 0.0 copy-done
  2.2 1.3 fusion.4
  3.5 0.3 copy.27
  3.8 34.1 %all_to_all.30 = f32[64,14,128]{2,1,0:T(8,128)S(1)} all-to-all(f32[64,14,128]{2,1,0:T(8,128)S(1)} %copy.27), channel_id=1, replica_groups=mesh['dp'=8,'fsdp'=8,'tensor'=8] {'dp','tensor'}, dimensions={0} | all-to-all | bytes 917504 | tf_op jit(solution)/shard_map/all_to_all | solution.py:39
  37.9 0.1 reduce_sum.45
  38.0 0.8 broadcast_in_dim.24
  38.8 6.7 %all-to-all-start.1 = ((f32[64,14,128]{2,1,0:T(8,128)}), f32[64,14,128]{2,1,0:T(8,128)S(1)}, u32[]{:S(2)}, u32[]{:S(2)}) async-start(f32[64,14,128]{2,1,0:T(8,128)} %broadcast_in_dim.24), calls=%async_computation.1 | async-start | bytes 1048576 | tf_op jit(solution)/shard_map/all_to_all | solution.py:43
  45.6 0.3 copy.28
  45.9 15.6 %all-to-all-done.1 = f32[64,14,128]{2,1,0:T(8,128)S(1)} async-done(((f32[64,14,128]{2,1,0:T(8,128)}), f32[64,14,128]{2,1,0:T(8,128)S(1)}, u32[]{:S(2)}, u32[]{:S(2)}) %all-to-all-start.1) | async-done | bytes 458784 | tf_op jit(solution)/shard_map/all_to_all | solution.py:43
  61.5 1.0 copy.29
  62.5 1.6 %fusion.20 = f32[8,16,128]{2,1,0:T(8,128)S(1)} fusion(f32[8,16,896]{2,1,0:T(8,128)} %bitcast.39, f32[896,128,1]{1,0,2:T(8,128)S(1)} %reshape.46), kind=kOutput, calls=%fused_computation.35 | convolution fusion | flops 176160768 | bytes 983040 | tf_op jit(solution)/shard_map/dot_general | solution.py:23
  64.1 0.9 fusion.19
  65.0 14.7 %all_to_all.31 = f32[8,48,128]{2,1,0:T(8,128)S(1)} all-to-all(f32[8,48,128]{2,1,0:T(8,128)S(1)} %pad_maximum_fusion), channel_id=1, replica_groups=mesh['dp'=8,'fsdp'=8,'tensor'=8] {'fsdp'}, dimensions={0} | all-to-all | bytes 393216 | tf_op jit(solution)/shard_map/all_to_all | solution.py:39
  79.7 0.0 copy-start.1
  79.7 0.7 broadcast_in_dim.25
  80.4 3.4 %all-to-all-start.3 = ((f32[8,32,128]{2,1,0:T(8,128)}), f32[8,32,128]{2,1,0:T(8,128)S(1)}, u32[]{:S(2)}, u32[]{:S(2)}) async-start(f32[8,32,128]{2,1,0:T(8,128)} %broadcast_in_dim.25), calls=%async_computation.3 | async-start | bytes 262144 | tf_op jit(solution)/shard_map/all_to_all | solution.py:43
  83.8 0.0 copy-done.1
  83.8 0.0 slice-start
  83.8 7.9 %all-to-all-done.3 = f32[8,32,128]{2,1,0:T(8,128)S(1)} async-done(((f32[8,32,128]{2,1,0:T(8,128)}), f32[8,32,128]{2,1,0:T(8,128)S(1)}, u32[]{:S(2)}, u32[]{:S(2)}) %all-to-all-start.3) | async-done | bytes 131104 | tf_op jit(solution)/shard_map/all_to_all | solution.py:43
  91.7 0.0 slice-done
  91.7 10.7 %all_to_all.32 = f32[8,48,128]{2,1,0:T(8,128)S(1)} all-to-all(f32[8,48,128]{2,1,0:T(8,128)S(1)} %broadcast_in_dim.26), channel_id=1, replica_groups=mesh['dp'=8,'fsdp'=8,'tensor'=8] {'fsdp'}, dimensions={0} | all-to-all | bytes 393216 | tf_op jit(solution)/shard_map/all_to_all | solution.py:43
  102.4 0.1 copy.30
  102.5 11.7 %cholesky.16 = f32[128,128]{1,0:T(8,128)S(1)} custom-call(f32[128,128]{1,0:T(8,128)S(1)} %fusion.16), custom_call_target="Cholesky" | custom-call | tf_op jit(solution)/shard_map/jit(cholesky)/cholesky | solution.py:61
  114.2 0.6 compare_reduce_fusion
  114.9 0.7 fusion.14
  115.6 9.8 %custom-call.7 = f32[1,128,128]{1,2,0:T(8,128)S(1)} custom-call(f32[1,128,128]{2,1,0:T(8,128)S(1)} %fusion.14), custom_call_target="InvertDiagBlocksLowerTriangular" | custom-call | tf_op jit(solution)/shard_map/jit(_solve_triangular)/triangular_solve | solution.py:35
  125.4 0.6 fusion.6
  126.1 0.6 broadcast_in_dim.28
  126.7 3.3 %all-to-all-start.5 = ((f32[8,1,128]{2,1,0:T(1,128)}), f32[8,1,128]{2,1,0:T(1,128)S(1)}, u32[]{:S(2)}, u32[]{:S(2)}) async-start(f32[8,1,128]{2,1,0:T(1,128)} %broadcast_in_dim.28), calls=%async_computation.5 | async-start | bytes 8192 | tf_op jit(solution)/shard_map/all_to_all | solution.py:43
  130.0 1.8 %fusion.1 = f32[1,1,896,256]{3,2,1,0:T(8,128)} fusion(f32[1,1,896,256]{3,2,1,0:T(8,128)S(1)} %convert_add_fusion, f32[1152,128]{1,0:T(8,128)S(1)} %fusion.6), kind=kOutput, calls=%fused_computation.3 | convolution fusion | flops 352780288 | bytes 2424832 | tf_op jit(solution)/shard_map/dot_general | solution.py:29
  131.8 4.6 %all-to-all-done.5 = f32[8,1,128]{2,1,0:T(1,128)S(1)} async-done(((f32[8,1,128]{2,1,0:T(1,128)}), f32[8,1,128]{2,1,0:T(1,128)S(1)}, u32[]{:S(2)}, u32[]{:S(2)}) %all-to-all-start.5) | async-done | bytes 4128 | tf_op jit(solution)/shard_map/all_to_all | solution.py:43
  136.4 1.7 %fusion.3 = bf16[1,896,256]{2,1,0:T(8,128)(2,1)} fusion(f32[1152,128]{1,0:T(8,128)S(1)} %fusion.6, f32[128]{0:T(128)S(1)} %sqrt_add_fusion), kind=kOutput, calls=%fused_computation.5 | convolution fusion | flops 352813056 | bytes 1049088 | tf_op jit(solution)/shard_map/dot_general | solution.py:29
  138.1 0.7 fusion.17
  (15 shorter events, 0.3 us)
Async XLA Ops:
  0.6 1.6 %copy-start = (f32[1,256,128]{2,1,0:T(8,128)S(1)}, f32[1,256,128]{2,1,0:T(8,128)}, u32[]{:S(2)}) copy-start(f32[1,256,128]{2,1,0:T(8,128)} %param.5) | copy-start | bytes 393220
  38.8 22.6 %all-to-all-start.1 = ((f32[64,14,128]{2,1,0:T(8,128)}), f32[64,14,128]{2,1,0:T(8,128)S(1)}, u32[]{:S(2)}, u32[]{:S(2)}) async-start(f32[64,14,128]{2,1,0:T(8,128)} %broadcast_in_dim.24), calls=%async_computation.1 | async-start | bytes 1048576 | tf_op jit(solution)/shard_map/all_to_all | solution.py:43
  79.7 4.1 %copy-start.1 = (f32[48,128]{1,0:T(8,128)}, f32[48,128]{1,0:T(8,128)S(1)}, u32[]{:S(2)}) copy-start(f32[48,128]{1,0:T(8,128)S(1)} %reduce_sum.46) | copy-start | bytes 73732
  80.4 11.3 %all-to-all-start.3 = ((f32[8,32,128]{2,1,0:T(8,128)}), f32[8,32,128]{2,1,0:T(8,128)S(1)}, u32[]{:S(2)}, u32[]{:S(2)}) async-start(f32[8,32,128]{2,1,0:T(8,128)} %broadcast_in_dim.25), calls=%async_computation.3 | async-start | bytes 262144 | tf_op jit(solution)/shard_map/all_to_all | solution.py:43
  83.8 7.9 %slice-start = ((f32[48,128]{1,0:T(8,128)}), f32[16,128]{1,0:T(8,128)S(1)}, s32[]{:S(2)}) async-start(f32[48,128]{1,0:T(8,128)} %copy-done.1), calls=%async_computation.6 | async-start | bytes 16384 | tf_op jit(solution)/shard_map/slice | solution.py:59
  126.7 9.7 %all-to-all-start.5 = ((f32[8,1,128]{2,1,0:T(1,128)}), f32[8,1,128]{2,1,0:T(1,128)S(1)}, u32[]{:S(2)}, u32[]{:S(2)}) async-start(f32[8,1,128]{2,1,0:T(1,128)} %broadcast_in_dim.28), calls=%async_computation.5 | async-start | bytes 8192 | tf_op jit(solution)/shard_map/all_to_all | solution.py:43

commit v2 on v1

--- a/solution.py
+++ b/solution.py
@@ -3,11 +3,14 @@
 import jax
 import jax.numpy as jnp
 from jax import lax
+from jax.experimental import pallas as pl
+from jax.experimental.pallas import tpu as pltpu
 from jax.sharding import PartitionSpec as P
 
 M_ROWS = 7168
 N_COLS = 2048
 RANK = 128
+SUB = 8
 
 
 highest = lax.Precision.HIGHEST
@@ -31,8 +34,63 @@
     )
 
 
-def whiten(matrix, factor_low):
-    return jax.scipy.linalg.solve_triangular(factor_low, matrix.T, lower=True).T
+def spread(row, count=SUB):
+    return jnp.broadcast_to(row, (count, RANK))
+
+def invert_factor(tiles, write):
+    lane = lax.broadcasted_iota(jnp.int32, (SUB, RANK), 1)
+    count = len(tiles)
+    for b in range(count):
+        first = b * SUB
+        panel = (lane >= first) & (lane < first + SUB)
+        below = range(b, count)
+        columns = {t: [jnp.broadcast_to(tiles[t][:, first + k:first + k + 1], (SUB, RANK)) for k in range(SUB)] for t in below}
+        pivot = [[spread(columns[b][j][k:k + 1]) if k >= j else None for k in range(SUB)] for j in range(SUB)]
+        rows = [jnp.where(panel, (lane == first + p).astype(jnp.float32), spread(tiles[b][p:p + 1])) for p in range(SUB)]
+        inverse = []
+        ratio = {}
+        for j in range(SUB):
+            inverse.append(1.0 / pivot[j][j])
+            for i in range(j + 1, SUB):
+                ratio[i, j] = pivot[j][i] * inverse[j]
+                for k in range(i, SUB):
+                    pivot[i][k] = pivot[i][k] - ratio[i, j] * pivot[j][k]
+                rows[i] = rows[i] - ratio[i, j] * rows[j]
+        for t in range(b + 1, count):
+            held = jnp.where(panel, 0.0, tiles[t])
+            left = columns[t]
+            for j in range(SUB):
+                multiple = left[j] * inverse[j]
+                for k in range(j + 1, SUB):
+                    left[k] = left[k] - multiple * pivot[j][k]
+                held = held - multiple * rows[j]
+            tiles[t] = held
+        for p in range(SUB):
+            d = pivot[p][p]
+            root = lax.rsqrt(d)
+            root = root * (1.5 - 0.5 * d * root * root)
+            write(first + p, jnp.where(lane <= first + p, rows[p] * root, 0.0)[0:1])
+
+def factor_kernel(parts_ref, out_ref):
+    tiles = [jnp.sum(parts_ref[:, t * SUB:(t + 1) * SUB, :], axis=0) for t in range(RANK // SUB)]
+
+    def write(row, value):
+        out_ref[row:row + 1, :] = value
+
+    invert_factor(tiles, write)
+
+
+def inverse_of_factor(parts):
+    count = parts.shape[0]
+    return pl.pallas_call(
+        factor_kernel,
+        grid=(1,),
+        out_shape=jax.ShapeDtypeStruct((RANK, RANK), jnp.float32),
+        in_specs=[pl.BlockSpec((count, RANK, RANK), lambda i: (0, 0, 0))],
+        out_specs=pl.BlockSpec((RANK, RANK), lambda i: (0, 0)),
+        compiler_params=pltpu.CompilerParams(vmem_limit_bytes=16 * 2**20),
+        cost_estimate=pl.CostEstimate(flops=4_000_000, bytes_accessed=4 * (count + 1) * RANK**2, transcendentals=0),
+    )(parts)
 
 
 def scatter_sum(blocks, axes):
@@ -51,21 +109,20 @@
     partial = product(blended, right_factor[0])
     part = scatter_sum(partial.reshape(plane, rows // plane, RANK), ("dp", "tensor"))
     projected = gather(part, ("dp", "tensor"), plane).reshape(rows, RANK)
-    right_raw = inner_rows(blended, projected).reshape(n_fsdp, cols // n_fsdp, RANK)
-    gram = inner_rows(projected, projected).reshape(n_fsdp, RANK // n_fsdp, RANK)
-    held = scatter_sum(jnp.concatenate([right_raw, gram], axis=1), "fsdp")
     own = cols // n_fsdp
-    summed = jnp.sum(gather(held[:own], "dp", n_dp), axis=0)
-    whole = gather(jnp.concatenate([summed, held[own:]], axis=0), "fsdp", n_fsdp)
-    right_raw = whole[:, :own].reshape(cols, RANK)
-    factor_low = jnp.linalg.cholesky(whole[:, own:].reshape(RANK, RANK))
-    both = whiten(jnp.concatenate([projected, right_raw / n_dp], axis=0), factor_low)
-    projected, reduced = both[:rows], both[rows:]
-    squares = jnp.sum(reduced * reduced, axis=0, keepdims=True)
-    squares = jnp.sum(gather(squares, "tensor", n_tensor), axis=0)
-    right_new = reduced / (jnp.sqrt(squares) + epsilon)
-    moment = blended - (1.0 - decay_rate) * outer_cols(projected, reduced)
-    direction = outer_cols(projected, right_new)
+    right_raw = inner_rows(blended, projected).reshape(n_fsdp, own, RANK)
+    gram = inner_rows(projected, projected)
+    sent = jnp.concatenate([jnp.broadcast_to(gram, (n_fsdp, RANK, RANK)), right_raw], axis=1)
+    parts = lax.all_to_all(sent, "fsdp", 0, 0)
+    replicas = gather(jnp.sum(parts[:, RANK:], axis=0), "dp", n_dp)
+    inverse_low = inverse_of_factor(parts)
+    reduced_own = outer_cols(jnp.sum(replicas, axis=0), inverse_low) / n_dp
+    reduced = gather(reduced_own, "fsdp", n_fsdp).reshape(cols, RANK)
+    squares = gather(jnp.sum(reduced_own * reduced_own, axis=0, keepdims=True), ("fsdp", "tensor"), n_fsdp * n_tensor)
+    orthonormal = outer_cols(projected, inverse_low)
+    moment = blended - (1.0 - decay_rate) * outer_cols(orthonormal, reduced)
+    right_new = reduced / (jnp.sqrt(jnp.sum(squares, axis=0)) + epsilon)
+    direction = outer_cols(orthonormal, right_new)
     update = (math.sqrt(M_ROWS * N_COLS / RANK) * direction).astype(jnp.bfloat16)
     return moment[None, None], right_new[None], update[None]
 

time: 139 us -> 127 us (0.914)
  other arithmetic: 25.2 us -> 2.27 us
  starting transfers between devices: 13.4 us -> 21.4 us
  blocking collectives: 59.5 us -> 53.8 us
  waiting for transfers between devices: 28 us -> 32.6 us
  Pallas kernels: 0 us -> 4.54 us
    another operation x5 -> x0, other arithmetic: 22.9 us -> none  [the longest x3 12.4 us: body(): factor_low = jnp.linalg.cholesky(whole[:, own:].reshape(RANK, RANK))]
    all_to_all x2 -> x1, blocking collectives: 48.8 us -> 34.1 us  [scatter_sum(): return jnp.sum(lax.all_to_all(blocks, axes, 0, 0), axis=0)]
    all_to_all x1, blocking collectives: 10.7 us -> 19.7 us  [body(): parts = lax.all_to_all(sent, 'fsdp', 0, 0)]
    all_to_all x3 -> x4, starting transfers between devices: 13.4 us -> 21.4 us  [gather(): lax.all_to_all(jnp.broadcast_to(block, (count,) + block.shape), axes, 0, 0)]
    all_to_all x3 -> x4, waiting for transfers between devices: 28 us -> 32.6 us  [gather(): lax.all_to_all(jnp.broadcast_to(block, (count,) + block.shape), axes, 0, 0)]
    pallas_call x0 -> x1, Pallas kernels: none -> 4.54 us  [inverse_of_factor(): pl.pallas_call(factor_kernel, grid=(1,), out_shape=jax.ShapeDtypeStruct((...]
    dot_general x2 -> x4, matrix products: 3.48 us -> 4.24 us  [outer_cols(): lax.dot_general(left, right, (((1,), (1,)), ((), ())), precision=highest,...]
  transfers between devices with their start and end apart: 3 -> 4, of which waited for: 3 -> 4; matrix products, arithmetic and copies ran while one was open for 2% -> 1% of each run, Pallas kernels for 0% -> 4%
where the time goes in v2:
time: 127 us; the launch traced here: 126 us
  blocking collectives  53.8 us (42%)
  waiting for transfers between devices  32.6 us (26%)
  starting transfers between devices  21.4 us (17%)
  matrix products  7.49 us (6%)
  Pallas kernels  4.54 us (4%)
  local copies, waits for them, and re-layouts  3.6 us (3%)
  other arithmetic  2.27 us (2%)
    all_to_all x1, blocking collectives, scatter_sum(): return jnp.sum(lax.all_to_all(blocks, axes, 0, 0), axis=0)  34.1 us
    all_to_all x4, waiting for transfers between devices, gather(): lax.all_to_all(jnp.broadcast_to(block, (count,) + block.shape), axes, 0, 0)  32.6 us
    all_to_all x4, starting transfers between devices, gather(): lax.all_to_all(jnp.broadcast_to(block, (count,) + block.shape), axes, 0, 0)  21.4 us
    all_to_all x1, blocking collectives, body(): parts = lax.all_to_all(sent, 'fsdp', 0, 0)  19.7 us
    pallas_call x1, Pallas kernels, inverse_of_factor(): pl.pallas_call(factor_kernel, grid=(1,), out_shape=jax.ShapeDtypeStruct((...  4.54 us
    dot_general x4, matrix products, outer_cols(): lax.dot_general(left, right, (((1,), (1,)), ((), ())), precision=highest,...  4.24 us
    broadcast_in_dim x4, local copies, waits for them, and re-layouts, gather(): jnp.broadcast_to(block, (count,) + block.shape)  2.8 us
  transfers between devices with their start and end apart: 4, of which 4 were waited for; matrix products, arithmetic and copies ran while one was open for 1% of the time, Pallas kernels for 4%

profile of v2, /device:TPU:1, one launch (start us, length us, event | category | flops | bytes accessed | tf_op | source)
XLA Modules:
  0.0 126.4 jit_solution(7944180515630928242)
XLA Ops:
  0.6 0.0 copy-start
  0.6 1.4 %convert_add_fusion = f32[1,1,896,256]{3,2,1,0:T(8,128)S(1)} fusion(f32[1,1,896,256]{3,2,1,0:T(8,128)} %param.3, bf16[1,1,896,256]{3,2,1,0:T(8,128)(2,1)} %param.4), kind=kLoop, calls=%fused_computation.10 | loop fusion | flops 458752 | bytes 2293760 | tf_op jit(solution)/shard_map/add | solution.py:106
  2.1 0.1 add.23
  2.2 0.0 copy-done
  2.2 1.3 %fusion.4 = f32[64,14,128]{2,0,1:T(8,128)S(1)} fusion(f32[64,14,256]{2,1,0:T(8,128)S(1)} %add.23, f32[1,256,128]{2,1,0:T(8,128)S(1)} %copy-done), kind=kOutput, calls=%fused_computation.8 | convolution fusion | flops 352321536 | bytes 1507328 | tf_op jit(solution)/shard_map/dot_general | solution.py:22
  3.5 0.3 copy.22
  3.8 34.1 %all_to_all.30 = f32[64,14,128]{2,1,0:T(8,128)S(1)} all-to-all(f32[64,14,128]{2,1,0:T(8,128)S(1)} %copy.22), channel_id=1, replica_groups=mesh['dp'=8,'fsdp'=8,'tensor'=8] {'dp','tensor'}, dimensions={0} | all-to-all | bytes 917504 | tf_op jit(solution)/shard_map/all_to_all | solution.py:97
  37.9 0.1 reduce_sum.45
  38.0 0.8 broadcast_in_dim.23
  38.8 6.7 %all-to-all-start.1 = ((f32[64,14,128]{2,1,0:T(8,128)}), f32[64,14,128]{2,1,0:T(8,128)S(1)}, u32[]{:S(2)}, u32[]{:S(2)}) async-start(f32[64,14,128]{2,1,0:T(8,128)} %broadcast_in_dim.23), calls=%async_computation.1 | async-start | bytes 1048576 | tf_op jit(solution)/shard_map/all_to_all | solution.py:101
  45.6 0.3 copy.25
  45.9 15.6 %all-to-all-done.1 = f32[64,14,128]{2,1,0:T(8,128)S(1)} async-done(((f32[64,14,128]{2,1,0:T(8,128)}), f32[64,14,128]{2,1,0:T(8,128)S(1)}, u32[]{:S(2)}, u32[]{:S(2)}) %all-to-all-start.1) | async-done | bytes 458784 | tf_op jit(solution)/shard_map/all_to_all | solution.py:101
  61.5 0.9 fusion.10
  62.4 1.0 convolution_bitcast_fusion
  63.6 19.7 %all_to_all.31.parts_ref = f32[8,160,128]{2,1,0:T(8,128)S(1)} all-to-all(f32[8,160,128]{2,1,0:T(8,128)S(1)} %pad_maximum_fusion), channel_id=1, replica_groups=mesh['dp'=8,'fsdp'=8,'tensor'=8] {'fsdp'}, dimensions={0} | all-to-all | bytes 1310720 | tf_op jit(solution)/shard_map/all_to_all | solution.py:116
  83.3 0.7 broadcast_in_dim.25
  83.9 3.4 %all-to-all-start.3 = ((f32[8,32,128]{2,1,0:T(8,128)}), f32[8,32,128]{2,1,0:T(8,128)S(1)}, u32[]{:S(2)}, u32[]{:S(2)}) async-start(f32[8,32,128]{2,1,0:T(8,128)} %broadcast_in_dim.25), calls=%async_computation.3 | async-start | bytes 262144 | tf_op jit(solution)/shard_map/all_to_all | solution.py:101
  87.4 4.5 %shard_map.58 = f32[128,128]{1,0:T(8,128)S(1)} custom-call(f32[8,160,128]{2,1,0:T(8,128)S(1)} %all_to_all.31.parts_ref), custom_call_target="tpu_custom_call" | custom-call | flops 4000000 | bytes 589824 | tf_op jit(solution)/shard_map/pallas_call | solution.py:85
  91.9 3.1 %all-to-all-done.3 = f32[8,32,128]{2,1,0:T(8,128)S(1)} async-done(((f32[8,32,128]{2,1,0:T(8,128)}), f32[8,32,128]{2,1,0:T(8,128)S(1)}, u32[]{:S(2)}, u32[]{:S(2)}) %all-to-all-start.3) | async-done | bytes 131104 | tf_op jit(solution)/shard_map/all_to_all | solution.py:101
  95.0 0.2 multiply_reduce_fusion
  95.3 0.6 broadcast_in_dim.28
  95.9 7.1 %all-to-all-start.5 = ((f32[64,1,128]{2,1,0:T(1,128)}), f32[64,1,128]{2,1,0:T(1,128)S(1)}, u32[]{:S(2)}, u32[]{:S(2)}) async-start(f32[64,1,128]{2,1,0:T(1,128)} %broadcast_in_dim.28), calls=%async_computation.5 | async-start | bytes 65536 | tf_op jit(solution)/shard_map/all_to_all | solution.py:101
  103.1 0.5 fusion.11
  103.6 8.6 %all-to-all-done.5 = f32[64,1,128]{2,1,0:T(1,128)S(1)} async-done(((f32[64,1,128]{2,1,0:T(1,128)}), f32[64,1,128]{2,1,0:T(1,128)S(1)}, u32[]{:S(2)}, u32[]{:S(2)}) %all-to-all-start.5) | async-done | bytes 32800 | tf_op jit(solution)/shard_map/all_to_all | solution.py:101
  112.2 0.7 broadcast_in_dim.26
  112.9 4.1 %all-to-all-start.4 = ((f32[8,32,128]{2,1,0:T(8,128)}), f32[8,32,128]{2,1,0:T(8,128)S(1)}, u32[]{:S(2)}, u32[]{:S(2)}) async-start(f32[8,32,128]{2,1,0:T(8,128)} %broadcast_in_dim.26), calls=%async_computation.4 | async-start | bytes 262144 | tf_op jit(solution)/shard_map/all_to_all | solution.py:101
  117.0 5.3 %all-to-all-done.4 = f32[8,32,128]{2,1,0:T(8,128)S(1)} async-done(((f32[8,32,128]{2,1,0:T(8,128)}), f32[8,32,128]{2,1,0:T(8,128)S(1)}, u32[]{:S(2)}, u32[]{:S(2)}) %all-to-all-start.4) | async-done | bytes 131104 | tf_op jit(solution)/shard_map/all_to_all | solution.py:101
  122.3 1.8 %fusion.1 = f32[1,1,896,256]{3,2,1,0:T(8,128)} fusion(f32[896,128]{1,0:T(8,128)S(1)} %fusion.11, f32[256,128]{1,0:T(8,128)S(1)} %bitcast.33, f32[1,1,896,256]{3,2,1,0:T(8,128)S(1)} %convert_add_fusion), kind=kOutput, calls=%fused_computation.3 | convolution fusion | flops 352780288 | bytes 2424832 | tf_op jit(solution)/shard_map/dot_general | solution.py:32
  124.1 1.7 %fusion.3 = bf16[1,896,256]{2,1,0:T(8,128)(2,1)} fusion(f32[896,128]{1,0:T(8,128)S(1)} %fusion.11, f32[256,128]{1,0:T(8,128)S(1)} %bitcast.34, f32[128]{0:T(128)S(1)} %sqrt_add_fusion), kind=kOutput, calls=%fused_computation.5 | convolution fusion | flops 352813056 | bytes 1049088 | tf_op jit(solution)/shard_map/dot_general | solution.py:32
  125.7 0.7 bitcast_divide_fusion
  (8 shorter events, 0.2 us)
Async XLA Ops:
  0.6 1.6 %copy-start = (f32[1,256,128]{2,1,0:T(8,128)S(1)}, f32[1,256,128]{2,1,0:T(8,128)}, u32[]{:S(2)}) copy-start(f32[1,256,128]{2,1,0:T(8,128)} %param.5) | copy-start | bytes 393220
  38.8 22.7 %all-to-all-start.1 = ((f32[64,14,128]{2,1,0:T(8,128)}), f32[64,14,128]{2,1,0:T(8,128)S(1)}, u32[]{:S(2)}, u32[]{:S(2)}) async-start(f32[64,14,128]{2,1,0:T(8,128)} %broadcast_in_dim.23), calls=%async_computation.1 | async-start | bytes 1048576 | tf_op jit(solution)/shard_map/all_to_all | solution.py:101
  83.9 11.1 %all-to-all-start.3 = ((f32[8,32,128]{2,1,0:T(8,128)}), f32[8,32,128]{2,1,0:T(8,128)S(1)}, u32[]{:S(2)}, u32[]{:S(2)}) async-start(f32[8,32,128]{2,1,0:T(8,128)} %broadcast_in_dim.25), calls=%async_computation.3 | async-start | bytes 262144 | tf_op jit(solution)/shard_map/all_to_all | solution.py:101
  95.9 16.3 %all-to-all-start.5 = ((f32[64,1,128]{2,1,0:T(1,128)}), f32[64,1,128]{2,1,0:T(1,128)S(1)}, u32[]{:S(2)}, u32[]{:S(2)}) async-start(f32[64,1,128]{2,1,0:T(1,128)} %broadcast_in_dim.28), calls=%async_computation.5 | async-start | bytes 65536 | tf_op jit(solution)/shard_map/all_to_all | solution.py:101
  112.9 9.4 %all-to-all-start.4 = ((f32[8,32,128]{2,1,0:T(8,128)}), f32[8,32,128]{2,1,0:T(8,128)S(1)}, u32[]{:S(2)}, u32[]{:S(2)}) async-start(f32[8,32,128]{2,1,0:T(8,128)} %broadcast_in_dim.26), calls=%async_computation.4 | async-start | bytes 262144 | tf_op jit(solution)/shard_map/all_to_all | solution.py:101

commit v3 on v2

--- a/solution.py
+++ b/solution.py
@@ -71,8 +71,9 @@
             root = root * (1.5 - 0.5 * d * root * root)
             write(first + p, jnp.where(lane <= first + p, rows[p] * root, 0.0)[0:1])
 
-def factor_kernel(parts_ref, out_ref):
-    tiles = [jnp.sum(parts_ref[:, t * SUB:(t + 1) * SUB, :], axis=0) for t in range(RANK // SUB)]
+def factor_kernel(upper_ref, lower_ref, out_ref):
+    half = RANK // 2
+    tiles = [ref[t:t + SUB, :] for ref in (upper_ref, lower_ref) for t in range(0, half, SUB)]
 
     def write(row, value):
         out_ref[row:row + 1, :] = value
@@ -80,17 +81,43 @@
     invert_factor(tiles, write)
 
 
-def inverse_of_factor(parts):
-    count = parts.shape[0]
+def inverse_of_factor(upper, lower):
     return pl.pallas_call(
         factor_kernel,
-        grid=(1,),
         out_shape=jax.ShapeDtypeStruct((RANK, RANK), jnp.float32),
-        in_specs=[pl.BlockSpec((count, RANK, RANK), lambda i: (0, 0, 0))],
-        out_specs=pl.BlockSpec((RANK, RANK), lambda i: (0, 0)),
+        in_specs=[pl.BlockSpec(memory_space=pltpu.VMEM)] * 2,
+        out_specs=pl.BlockSpec(memory_space=pltpu.VMEM),
         compiler_params=pltpu.CompilerParams(vmem_limit_bytes=16 * 2**20),
-        cost_estimate=pl.CostEstimate(flops=4_000_000, bytes_accessed=4 * (count + 1) * RANK**2, transcendentals=0),
-    )(parts)
+        cost_estimate=pl.CostEstimate(flops=4_000_000, bytes_accessed=8 * RANK**2, transcendentals=0),
+    )(upper, lower)
+
+
+def inner_kernel(blended_ref, projected_ref, out_ref):
+    count, high, _ = out_ref.shape
+    half = RANK // 2
+    own = high - half
+    projected = projected_ref[...]
+    flipped = projected.T
+    right_raw = product(flipped, blended_ref[...]).T
+    gram = product(flipped, projected)
+    for k in range(count):
+        out_ref[k, :own] = right_raw[k * own:(k + 1) * own]
+        out_ref[k, own:] = gram[k % 2 * half:(k % 2 + 1) * half]
+
+
+def inner_products(blended, projected, count):
+    rows, cols = blended.shape
+    high = cols // count + RANK // 2
+    return pl.pallas_call(
+        inner_kernel,
+        out_shape=jax.ShapeDtypeStruct((count, high, RANK), jnp.float32),
+        in_specs=[pl.BlockSpec(memory_space=pltpu.VMEM)] * 2,
+        out_specs=pl.BlockSpec(memory_space=pltpu.VMEM),
+        compiler_params=pltpu.CompilerParams(vmem_limit_bytes=24 * 2**20),
+        cost_estimate=pl.CostEstimate(
+            flops=2 * rows * (cols + RANK) * RANK, bytes_accessed=4 * rows * (cols + RANK), transcendentals=0
+        ),
+    )(blended, projected)
 
 
 def scatter_sum(blocks, axes):
@@ -110,16 +137,17 @@
     part = scatter_sum(partial.reshape(plane, rows // plane, RANK), ("dp", "tensor"))
     projected = gather(part, ("dp", "tensor"), plane).reshape(rows, RANK)
     own = cols // n_fsdp
-    right_raw = inner_rows(blended, projected).reshape(n_fsdp, own, RANK)
-    gram = inner_rows(projected, projected)
-    sent = jnp.concatenate([jnp.broadcast_to(gram, (n_fsdp, RANK, RANK)), right_raw], axis=1)
-    parts = lax.all_to_all(sent, "fsdp", 0, 0)
-    replicas = gather(jnp.sum(parts[:, RANK:], axis=0), "dp", n_dp)
-    inverse_low = inverse_of_factor(parts)
+    parts = scatter_sum(inner_products(blended, projected, n_fsdp), "fsdp")
+    replicas = gather(parts[:own], "dp", n_dp)
+    mine = parts[own:]
+    other = lax.ppermute(mine, "fsdp", [(k, k ^ 1) for k in range(n_fsdp)])
+    even = lax.axis_index("fsdp") % 2 == 0
+    inverse_low = inverse_of_factor(jnp.where(even, mine, other), jnp.where(even, other, mine))
+    orthonormal = outer_cols(projected, inverse_low)
+    replicas, orthonormal = lax.optimization_barrier((replicas, orthonormal))
     reduced_own = outer_cols(jnp.sum(replicas, axis=0), inverse_low) / n_dp
     reduced = gather(reduced_own, "fsdp", n_fsdp).reshape(cols, RANK)
-    squares = gather(jnp.sum(reduced_own * reduced_own, axis=0, keepdims=True), ("fsdp", "tensor"), n_fsdp * n_tensor)
-    orthonormal = outer_cols(projected, inverse_low)
+    squares = gather(jnp.sum(reduced * reduced, axis=0, keepdims=True), "tensor", n_tensor)
     moment = blended - (1.0 - decay_rate) * outer_cols(orthonormal, reduced)
     right_new = reduced / (jnp.sqrt(jnp.sum(squares, axis=0)) + epsilon)
     direction = outer_cols(orthonormal, right_new)

time: 127 us -> 117 us (0.921)
  blocking collectives: 53.8 us -> 82.6 us
  waiting for transfers between devices: 32.6 us -> 7.99 us
  starting transfers between devices: 21.4 us -> 9.57 us
  matrix products: 7.49 us -> 5.51 us
  local copies, waits for them, and re-layouts: 3.6 us -> 1.77 us
    all_to_all x4 -> x2, waiting for transfers between devices: 32.6 us -> 7.99 us  [gather(): lax.all_to_all(jnp.broadcast_to(block, (count,) + block.shape), axes, 0, 0)]
    all_to_all x1 -> x2, blocking collectives: 34.1 us -> 51 us  [scatter_sum(): return jnp.sum(lax.all_to_all(blocks, axes, 0, 0), axis=0)]
    all_to_all x4 -> x2, starting transfers between devices: 21.4 us -> 6.8 us  [gather(): lax.all_to_all(jnp.broadcast_to(block, (count,) + block.shape), axes, 0, 0)]
    all_to_all x1 -> x2, blocking collectives: 19.7 us -> 31.6 us  [gather(): lax.all_to_all(jnp.broadcast_to(block, (count,) + block.shape), axes, 0, 0)]
    ppermute x0 -> x1, starting transfers between devices: none -> 2.77 us  [body(): other = lax.ppermute(mine, 'fsdp', [(k, k ^ 1) for k in range(n_fsdp)])]
    dot_general x2 -> x0, matrix products: 1.95 us -> none  [inner_rows(): lax.dot_general(left, right, (((0,), (0,)), ((), ())), precision=highest,...]
    broadcast_in_dim x4, local copies, waits for them, and re-layouts: 2.8 us -> 1.33 us  [gather(): jnp.broadcast_to(block, (count,) + block.shape)]
    pallas_call x1 -> x2, Pallas kernels: 4.54 us -> 5.66 us  [the longest x1 4.53 us: inverse_of_factor(): pl.pallas_call(factor_kernel, out_shape=jax.ShapeDtypeStruct((RANK, RANK)...]
  transfers between devices with their start and end apart: 4 -> 3, of which waited for: 4 -> 2; matrix products, arithmetic and copies ran while one was open for 1% -> 3% of each run, Pallas kernels for 4% -> 4%
where the time goes in v3:
time: 117 us; the launch traced here: 116 us
  blocking collectives  82.6 us (71%)
  starting transfers between devices  9.57 us (8%)
  waiting for transfers between devices  7.99 us (7%)
  Pallas kernels  5.66 us (5%)
  matrix products  5.51 us (5%)
  other arithmetic  2.29 us (2%)
  local copies, waits for them, and re-layouts  1.77 us (2%)
    all_to_all x2, blocking collectives, scatter_sum(): return jnp.sum(lax.all_to_all(blocks, axes, 0, 0), axis=0)  51 us
    all_to_all x2, blocking collectives, gather(): lax.all_to_all(jnp.broadcast_to(block, (count,) + block.shape), axes, 0, 0)  31.6 us
    all_to_all x2, waiting for transfers between devices, gather(): lax.all_to_all(jnp.broadcast_to(block, (count,) + block.shape), axes, 0, 0)  7.99 us
    all_to_all x2, starting transfers between devices, gather(): lax.all_to_all(jnp.broadcast_to(block, (count,) + block.shape), axes, 0, 0)  6.8 us
    pallas_call x1, Pallas kernels, inverse_of_factor(): pl.pallas_call(factor_kernel, out_shape=jax.ShapeDtypeStruct((RANK, RANK)...  4.53 us
    dot_general x4, matrix products, outer_cols(): lax.dot_general(left, right, (((1,), (1,)), ((), ())), precision=highest,...  4.21 us
    ppermute x1, starting transfers between devices, body(): other = lax.ppermute(mine, 'fsdp', [(k, k ^ 1) for k in range(n_fsdp)])  2.77 us
  transfers between devices with their start and end apart: 3, of which 2 were waited for; matrix products, arithmetic and copies ran while one was open for 3% of the time, Pallas kernels for 4%

profile of v3, /device:TPU:1, one launch (start us, length us, event | category | flops | bytes accessed | tf_op | source)
XLA Modules:
  0.0 116.2 jit_solution(2571623318814408880)
XLA Ops:
  0.6 0.0 copy-start
  0.6 1.4 %convert_add_fusion = f32[1,1,896,256]{3,2,1,0:T(8,128)S(1)} fusion(f32[1,1,896,256]{3,2,1,0:T(8,128)} %param.3, bf16[1,1,896,256]{3,2,1,0:T(8,128)(2,1)} %param.4), kind=kLoop, calls=%fused_computation.9 | loop fusion | flops 458752 | bytes 2293760 | tf_op jit(solution)/shard_map/add | solution.py:133
  2.1 0.1 add.24
  2.2 0.0 copy-done
  2.2 1.3 %fusion.4 = f32[64,14,128]{2,0,1:T(8,128)S(1)} fusion(f32[64,14,256]{2,1,0:T(8,128)S(1)} %add.24, f32[1,256,128]{2,1,0:T(8,128)S(1)} %copy-done), kind=kOutput, calls=%fused_computation.7 | convolution fusion | flops 352321536 | bytes 1507328 | tf_op jit(solution)/shard_map/dot_general | solution.py:22
  3.5 0.3 copy.13
  3.8 34.1 %all_to_all.30 = f32[64,14,128]{2,1,0:T(8,128)S(1)} all-to-all(f32[64,14,128]{2,1,0:T(8,128)S(1)} %copy.13), channel_id=1, replica_groups=mesh['dp'=8,'fsdp'=8,'tensor'=8] {'dp','tensor'}, dimensions={0} | all-to-all | bytes 917504 | tf_op jit(solution)/shard_map/all_to_all | solution.py:124
  37.9 0.1 reduce_sum.45
  38.0 22.4 %all_to_all.31 = f32[64,14,128]{2,1,0:T(8,128)S(1)} all-to-all(f32[64,14,128]{2,1,0:T(8,128)S(1)} %broadcast_in_dim.20), channel_id=1, replica_groups=mesh['dp'=8,'fsdp'=8,'tensor'=8] {'dp','tensor'}, dimensions={0} | all-to-all | bytes 917504 | tf_op jit(solution)/shard_map/all_to_all | solution.py:128
  60.5 1.1 shard_map.58
  61.6 16.9 %all_to_all.32 = f32[8,96,128]{2,1,0:T(8,128)S(1)} all-to-all(f32[8,96,128]{2,1,0:T(8,128)S(1)} %shard_map.58), channel_id=1, replica_groups=mesh['dp'=8,'fsdp'=8,'tensor'=8] {'fsdp'}, dimensions={0} | all-to-all | bytes 786432 | tf_op jit(solution)/shard_map/all_to_all | solution.py:124
  78.5 2.8 %collective-permute-start = (f32[64,128]{1,0:T(8,128)S(1)}, f32[64,128]{1,0:T(8,128)S(1)}, u32[]{:S(2)}, u32[]{:S(2)}) collective-permute-start(f32[64,128]{1,0:T(8,128)S(1)} %slice.9), channel_id=1, source_target_pairs={{0,8},{8,0},{16,24},{24,16},{32,40},{40,32},{48,56},{56,48},{1,9},... | collective-permute-start | bytes 98312 | tf_op jit(solution)/shard_map/ppermute | solution.py:143
  81.3 0.7 broadcast_in_dim.21
  82.0 3.4 %all-to-all-start.3 = ((f32[8,32,128]{2,1,0:T(8,128)}), f32[8,32,128]{2,1,0:T(8,128)S(1)}, u32[]{:S(2)}, u32[]{:S(2)}) async-start(f32[8,32,128]{2,1,0:T(8,128)} %broadcast_in_dim.21), calls=%async_computation.3 | async-start | bytes 262144 | tf_op jit(solution)/shard_map/all_to_all | solution.py:128
  85.4 0.0 collective-permute-done
  85.4 4.5 %shard_map.59 = f32[128,128]{1,0:T(8,128)S(1)} custom-call(f32[64,128]{1,0:T(8,128)S(1)} %get-tuple-element.8.upper_ref, f32[64,128]{1,0:T(8,128)S(1)} %get-tuple-element.7.lower_ref), custom_call_target="tpu_custom_call" | custom-call | flops 4000000 | bytes 131072 | tf_op jit(solution)/shard_map/pallas_call | solution.py:85
  89.9 0.5 fusion.9
  90.5 3.3 %all-to-all-done.3 = f32[8,32,128]{2,1,0:T(8,128)S(1)} async-done(((f32[8,32,128]{2,1,0:T(8,128)}), f32[8,32,128]{2,1,0:T(8,128)S(1)}, u32[]{:S(2)}, u32[]{:S(2)}) %all-to-all-start.3) | async-done | bytes 131104 | tf_op jit(solution)/shard_map/all_to_all | solution.py:128
  93.8 0.2 convolution_multiply_fusion.2
  94.1 9.2 %all_to_all.33 = f32[8,32,128]{2,1,0:T(8,128)S(1)} all-to-all(f32[8,32,128]{2,1,0:T(8,128)S(1)} %broadcast_in_dim.22), channel_id=1, replica_groups=mesh['dp'=8,'fsdp'=8,'tensor'=8] {'fsdp'}, dimensions={0} | all-to-all | bytes 262144 | tf_op jit(solution)/shard_map/all_to_all | solution.py:128
  103.3 0.6 broadcast_in_dim.24
  103.9 3.4 %all-to-all-start.5 = ((f32[8,1,128]{2,1,0:T(1,128)}), f32[8,1,128]{2,1,0:T(1,128)S(1)}, u32[]{:S(2)}, u32[]{:S(2)}) async-start(f32[8,1,128]{2,1,0:T(1,128)} %broadcast_in_dim.24), calls=%async_computation.5 | async-start | bytes 8192 | tf_op jit(solution)/shard_map/all_to_all | solution.py:128
  107.3 1.8 %fusion.1 = f32[1,1,896,256]{3,2,1,0:T(8,128)} fusion(f32[896,128]{1,0:T(8,128)S(1)} %fusion.9, f32[256,128]{1,0:T(8,128)S(1)} %bitcast.25, f32[1,1,896,256]{3,2,1,0:T(8,128)S(1)} %convert_add_fusion), kind=kOutput, calls=%fused_computation.3 | convolution fusion | flops 352780288 | bytes 2424832 | tf_op jit(solution)/shard_map/dot_general | solution.py:32
  109.1 4.6 %all-to-all-done.5 = f32[8,1,128]{2,1,0:T(1,128)S(1)} async-done(((f32[8,1,128]{2,1,0:T(1,128)}), f32[8,1,128]{2,1,0:T(1,128)S(1)}, u32[]{:S(2)}, u32[]{:S(2)}) %all-to-all-start.5) | async-done | bytes 4128 | tf_op jit(solution)/shard_map/all_to_all | solution.py:128
  113.8 1.7 %fusion.3 = bf16[1,896,256]{2,1,0:T(8,128)(2,1)} fusion(f32[896,128]{1,0:T(8,128)S(1)} %fusion.9, f32[256,128]{1,0:T(8,128)S(1)} %bitcast.26, f32[128]{0:T(128)S(1)} %sqrt_add_fusion), kind=kOutput, calls=%fused_computation.5 | convolution fusion | flops 352813056 | bytes 1049088 | tf_op jit(solution)/shard_map/dot_general | solution.py:32
  115.5 0.7 bitcast_divide_fusion
  (11 shorter events, 0.2 us)
Async XLA Ops:
  0.6 1.6 %copy-start = (f32[1,256,128]{2,1,0:T(8,128)S(1)}, f32[1,256,128]{2,1,0:T(8,128)}, u32[]{:S(2)}) copy-start(f32[1,256,128]{2,1,0:T(8,128)} %param.5) | copy-start | bytes 393220
  78.5 6.9 %collective-permute-start = (f32[64,128]{1,0:T(8,128)S(1)}, f32[64,128]{1,0:T(8,128)S(1)}, u32[]{:S(2)}, u32[]{:S(2)}) collective-permute-start(f32[64,128]{1,0:T(8,128)S(1)} %slice.9), channel_id=1, source_target_pairs={{0,8},{8,0},{16,24},{24,16},{32,40},{40,32},{48,56},{56,48},{1,9},... | collective-permute-start | bytes 98312 | tf_op jit(solution)/shard_map/ppermute | solution.py:143
  82.0 11.8 %all-to-all-start.3 = ((f32[8,32,128]{2,1,0:T(8,128)}), f32[8,32,128]{2,1,0:T(8,128)S(1)}, u32[]{:S(2)}, u32[]{:S(2)}) async-start(f32[8,32,128]{2,1,0:T(8,128)} %broadcast_in_dim.21), calls=%async_computation.3 | async-start | bytes 262144 | tf_op jit(solution)/shard_map/all_to_all | solution.py:128
  103.9 9.9 %all-to-all-start.5 = ((f32[8,1,128]{2,1,0:T(1,128)}), f32[8,1,128]{2,1,0:T(1,128)S(1)}, u32[]{:S(2)}, u32[]{:S(2)}) async-start(f32[8,1,128]{2,1,0:T(1,128)} %broadcast_in_dim.24), calls=%async_computation.5 | async-start | bytes 8192 | tf_op jit(solution)/shard_map/all_to_all | solution.py:128

commit v4 on v3

--- a/solution.py
+++ b/solution.py
@@ -11,6 +11,7 @@
 N_COLS = 2048
 RANK = 128
 SUB = 8
+REPLICAS = 8
 
 
 highest = lax.Precision.HIGHEST
@@ -71,53 +72,114 @@
             root = root * (1.5 - 0.5 * d * root * root)
             write(first + p, jnp.where(lane <= first + p, rows[p] * root, 0.0)[0:1])
 
-def factor_kernel(upper_ref, lower_ref, out_ref):
-    half = RANK // 2
-    tiles = [ref[t:t + SUB, :] for ref in (upper_ref, lower_ref) for t in range(0, half, SUB)]
+def whiten_kernel(whole_ref, inverse_ref, reduced_ref, squares_ref):
+    count, high, _ = whole_ref.shape
+    share = RANK // count
+    own = high - share
+    tiles = [whole_ref[k, t:t + SUB] for k in range(count) for t in range(own, high, SUB)]
 
     def write(row, value):
-        out_ref[row:row + 1, :] = value
+        inverse_ref[row:row + 1, :] = value
 
     invert_factor(tiles, write)
-
-
-def inverse_of_factor(upper, lower):
+    right_raw = jnp.concatenate([whole_ref[k, :own] for k in range(count)], axis=0)
+    reduced = outer_cols(right_raw, inverse_ref[...]) * (1.0 / REPLICAS)
+    reduced_ref[...] = reduced
+    squares = jnp.sum(reduced * reduced, axis=0, keepdims=True)
+    for k in range(squares_ref.shape[0]):
+        squares_ref[k] = squares
+
+
+def whiten_right(whole, n_tensor):
+    count, high, _ = whole.shape
+    cols = count * high - RANK
+    vmem = pl.BlockSpec(memory_space=pltpu.VMEM)
     return pl.pallas_call(
-        factor_kernel,
-        out_shape=jax.ShapeDtypeStruct((RANK, RANK), jnp.float32),
-        in_specs=[pl.BlockSpec(memory_space=pltpu.VMEM)] * 2,
-        out_specs=pl.BlockSpec(memory_space=pltpu.VMEM),
+        whiten_kernel,
+        out_shape=(
+            jax.ShapeDtypeStruct((RANK, RANK), jnp.float32),
+            jax.ShapeDtypeStruct((cols, RANK), jnp.float32),
+            jax.ShapeDtypeStruct((n_tensor, 1, RANK), jnp.float32),
+        ),
+        in_specs=[vmem],
+        out_specs=[vmem] * 3,
         compiler_params=pltpu.CompilerParams(vmem_limit_bytes=16 * 2**20),
-        cost_estimate=pl.CostEstimate(flops=4_000_000, bytes_accessed=8 * RANK**2, transcendentals=0),
-    )(upper, lower)
+    )(whole)
 
 
 def inner_kernel(blended_ref, projected_ref, out_ref):
     count, high, _ = out_ref.shape
-    half = RANK // 2
-    own = high - half
+    share = RANK // count
+    own = high - share
     projected = projected_ref[...]
     flipped = projected.T
     right_raw = product(flipped, blended_ref[...]).T
     gram = product(flipped, projected)
     for k in range(count):
         out_ref[k, :own] = right_raw[k * own:(k + 1) * own]
-        out_ref[k, own:] = gram[k % 2 * half:(k % 2 + 1) * half]
+        out_ref[k, own:] = gram[k * share:(k + 1) * share]
 
 
 def inner_products(blended, projected, count):
     rows, cols = blended.shape
-    high = cols // count + RANK // 2
+    vmem = pl.BlockSpec(memory_space=pltpu.VMEM)
     return pl.pallas_call(
         inner_kernel,
-        out_shape=jax.ShapeDtypeStruct((count, high, RANK), jnp.float32),
-        in_specs=[pl.BlockSpec(memory_space=pltpu.VMEM)] * 2,
-        out_specs=pl.BlockSpec(memory_space=pltpu.VMEM),
+        out_shape=jax.ShapeDtypeStruct((count, (cols + RANK) // count, RANK), jnp.float32),
+        in_specs=[vmem] * 2,
+        out_specs=vmem,
         compiler_params=pltpu.CompilerParams(vmem_limit_bytes=24 * 2**20),
-        cost_estimate=pl.CostEstimate(
-            flops=2 * rows * (cols + RANK) * RANK, bytes_accessed=4 * rows * (cols + RANK), transcendentals=0
+    )(blended, projected)
+
+
+def halves(x):
+    high = x.astype(jnp.bfloat16)
+    return high, (x - high.astype(jnp.float32)).astype(jnp.bfloat16)
+
+
+def update_kernel(left_ref, reduced_ref, squares_ref, right_out, update_out, right_ref, update_ref, sems):
+    steps = sems.shape[0] - 1
+    rows = left_ref.shape[0] // steps
+
+    def outer(left, right):
+        return lax.dot_general(left, right, (((1,), (1,)), ((), ())), preferred_element_type=jnp.float32)
+
+    norm = jnp.sqrt(jnp.sum(squares_ref[...], axis=0)) + epsilon
+    right_new = reduced_ref[...] / norm
+    right_ref[...] = right_new
+    copies = [pltpu.make_async_copy(right_ref, right_out, sems.at[steps])]
+    copies[0].start()
+    right_high, right_low = halves(right_new * math.sqrt(M_ROWS * N_COLS / RANK))
+    for step in range(steps):
+        block = pl.ds(step * rows, rows)
+        left_high, left_low = halves(left_ref[block, :])
+        total = outer(left_high, right_high) + (outer(left_high, right_low) + outer(left_low, right_high))
+        update_ref[block, :] = total.astype(jnp.bfloat16)
+        copies.append(pltpu.make_async_copy(update_ref.at[block], update_out.at[block], sems.at[step]))
+        copies[-1].start()
+    for copy in copies:
+        copy.wait()
+
+
+def update_and_right(left, reduced, squares):
+    steps = 4
+    rows, cols = left.shape[0], reduced.shape[0]
+    vmem, anywhere = pl.BlockSpec(memory_space=pltpu.VMEM), pl.BlockSpec(memory_space=pl.ANY)
+    return pl.pallas_call(
+        update_kernel,
+        out_shape=(
+            jax.ShapeDtypeStruct((cols, RANK), jnp.float32),
+            jax.ShapeDtypeStruct((rows, cols), jnp.bfloat16),
         ),
-    )(blended, projected)
+        in_specs=[vmem] * 3,
+        out_specs=[anywhere] * 2,
+        scratch_shapes=[
+            pltpu.VMEM((cols, RANK), jnp.float32),
+            pltpu.VMEM((rows, cols), jnp.bfloat16),
+            pltpu.SemaphoreType.DMA((steps + 1,)),
+        ],
+        compiler_params=pltpu.CompilerParams(vmem_limit_bytes=16 * 2**20),
+    )(left, reduced, squares)
 
 
 def scatter_sum(blocks, axes):
@@ -133,25 +195,18 @@
     blended = momentum[0, 0] + gradient[0, 0].astype(jnp.float32)
     rows, cols = blended.shape
     plane = n_dp * n_tensor
-    partial = product(blended, right_factor[0])
+    partial = lax.optimization_barrier(product(blended, right_factor[0]))
     part = scatter_sum(partial.reshape(plane, rows // plane, RANK), ("dp", "tensor"))
     projected = gather(part, ("dp", "tensor"), plane).reshape(rows, RANK)
     own = cols // n_fsdp
-    parts = scatter_sum(inner_products(blended, projected, n_fsdp), "fsdp")
-    replicas = gather(parts[:own], "dp", n_dp)
-    mine = parts[own:]
-    other = lax.ppermute(mine, "fsdp", [(k, k ^ 1) for k in range(n_fsdp)])
-    even = lax.axis_index("fsdp") % 2 == 0
-    inverse_low = inverse_of_factor(jnp.where(even, mine, other), jnp.where(even, other, mine))
+    held = scatter_sum(inner_products(blended, projected, n_fsdp), "fsdp")
+    summed = jnp.sum(gather(held[:own], "dp", n_dp), axis=0)
+    whole = gather(jnp.concatenate([summed, held[own:]], axis=0), "fsdp", n_fsdp)
+    inverse_low, reduced, squares = whiten_right(whole, n_tensor)
+    squares = lax.all_to_all(squares, "tensor", 0, 0)
     orthonormal = outer_cols(projected, inverse_low)
-    replicas, orthonormal = lax.optimization_barrier((replicas, orthonormal))
-    reduced_own = outer_cols(jnp.sum(replicas, axis=0), inverse_low) / n_dp
-    reduced = gather(reduced_own, "fsdp", n_fsdp).reshape(cols, RANK)
-    squares = gather(jnp.sum(reduced * reduced, axis=0, keepdims=True), "tensor", n_tensor)
     moment = blended - (1.0 - decay_rate) * outer_cols(orthonormal, reduced)
-    right_new = reduced / (jnp.sqrt(jnp.sum(squares, axis=0)) + epsilon)
-    direction = outer_cols(orthonormal, right_new)
-    update = (math.sqrt(M_ROWS * N_COLS / RANK) * direction).astype(jnp.bfloat16)
+    right_new, update = update_and_right(orthonormal, reduced, squares)
     return moment[None, None], right_new[None], update[None]
 
 

time: 117 us -> 116 us (level)
  waiting for transfers between devices: 7.99 us -> 12.4 us
  starting transfers between devices: 9.57 us -> 6.69 us
  matrix products: 5.51 us -> 3.23 us
  Pallas kernels: 5.66 us -> 7.81 us
    all_to_all x0 -> x1, waiting for transfers between devices: none -> 4.56 us  [body(): squares = lax.all_to_all(squares, 'tensor', 0, 0)]
    all_to_all x2 -> x1, starting transfers between devices: 6.8 us -> 3.37 us  [gather(): lax.all_to_all(jnp.broadcast_to(block, (count,) + block.shape), axes, 0, 0)]
    all_to_all x0 -> x1, starting transfers between devices: none -> 3.32 us  [body(): squares = lax.all_to_all(squares, 'tensor', 0, 0)]
    ppermute x1 -> x0, starting transfers between devices: 2.77 us -> none  [body(): other = lax.ppermute(mine, 'fsdp', [(k, k ^ 1) for k in range(n_fsdp)])]
    all_to_all x2, blocking collectives: 51 us -> 48.7 us  [scatter_sum(): return jnp.sum(lax.all_to_all(blocks, axes, 0, 0), axis=0)]
    pallas_call x2 -> x3, Pallas kernels: 5.66 us -> 7.81 us  [the longest x1 5.39 us: whiten_right(): pl.pallas_call(whiten_kernel, out_shape=(jax.ShapeDtypeStruct((RANK, RANK...]
    dot_general x4 -> x2, matrix products: 4.21 us -> 2.34 us  [outer_cols(): lax.dot_general(left, right, (((1,), (1,)), ((), ())), precision=highest,...]
    all_to_all x2, blocking collectives: 31.6 us -> 33.1 us  [gather(): lax.all_to_all(jnp.broadcast_to(block, (count,) + block.shape), axes, 0, 0)]
  transfers between devices with their start and end apart: 3 -> 2, of which waited for: 2 -> 2; matrix products, arithmetic and copies ran while one was open for 3% -> 2% of each run, Pallas kernels for 4% -> 0%
where the time goes in v4:
time: 116 us; the launch traced here: 115 us
  blocking collectives  81.9 us (71%)
  waiting for transfers between devices  12.4 us (11%)
  Pallas kernels  7.81 us (7%)
  starting transfers between devices  6.69 us (6%)
  matrix products  3.23 us (3%)
  other arithmetic  1.53 us (1%)
    all_to_all x2, blocking collectives, scatter_sum(): return jnp.sum(lax.all_to_all(blocks, axes, 0, 0), axis=0)  48.7 us
    all_to_all x2, blocking collectives, gather(): lax.all_to_all(jnp.broadcast_to(block, (count,) + block.shape), axes, 0, 0)  33.1 us
    all_to_all x1, waiting for transfers between devices, gather(): lax.all_to_all(jnp.broadcast_to(block, (count,) + block.shape), axes, 0, 0)  7.84 us
    pallas_call x1, Pallas kernels, whiten_right(): pl.pallas_call(whiten_kernel, out_shape=(jax.ShapeDtypeStruct((RANK, RANK...  5.39 us
    all_to_all x1, waiting for transfers between devices, body(): squares = lax.all_to_all(squares, 'tensor', 0, 0)  4.56 us
    all_to_all x1, starting transfers between devices, gather(): lax.all_to_all(jnp.broadcast_to(block, (count,) + block.shape), axes, 0, 0)  3.37 us
    all_to_all x1, starting transfers between devices, body(): squares = lax.all_to_all(squares, 'tensor', 0, 0)  3.32 us
    dot_general x2, matrix products, outer_cols(): lax.dot_general(left, right, (((1,), (1,)), ((), ())), precision=highest,...  2.34 us
  transfers between devices with their start and end apart: 2, of which 2 were waited for; matrix products, arithmetic and copies ran while one was open for 2% of the time, Pallas kernels for 0%

profile of v4, /device:TPU:1, one launch (start us, length us, event | category | flops | bytes accessed | tf_op | source)
XLA Modules:
  0.0 115.1 jit_solution(16080520366661577721)
XLA Ops:
  0.6 0.0 copy-start
  0.6 1.4 %add_bitcast_fusion.blended_ref = f32[896,256]{1,0:T(8,128)S(1)} fusion(f32[1,1,896,256]{3,2,1,0:T(8,128)} %param.3, bf16[1,1,896,256]{3,2,1,0:T(8,128)(2,1)} %param.4), kind=kLoop, calls=%fused_computation.3 | loop fusion | flops 458752 | bytes 2293760 | tf_op jit(solution)/shard_map/add | solution.py:195
  2.1 0.0 copy-done
  2.1 0.9 fusion.2
  3.0 34.1 %all_to_all.30 = f32[64,14,128]{2,1,0:T(8,128)S(1)} all-to-all(f32[64,14,128]{2,1,0:T(8,128)S(1)} %reshape.15), channel_id=1, replica_groups=mesh['dp'=8,'fsdp'=8,'tensor'=8] {'dp','tensor'}, dimensions={0} | all-to-all | bytes 917504 | tf_op jit(solution)/shard_map/all_to_all | solution.py:186
  37.1 0.1 reduce_sum.27
  37.2 22.5 %all_to_all.31 = f32[64,14,128]{2,1,0:T(8,128)S(1)} all-to-all(f32[64,14,128]{2,1,0:T(8,128)S(1)} %broadcast_in_dim.18), channel_id=1, replica_groups=mesh['dp'=8,'fsdp'=8,'tensor'=8] {'dp','tensor'}, dimensions={0} | all-to-all | bytes 917504 | tf_op jit(solution)/shard_map/all_to_all | solution.py:190
  59.8 1.1 shard_map.58
  60.9 14.6 %all_to_all.32 = f32[8,48,128]{2,1,0:T(8,128)S(1)} all-to-all(f32[8,48,128]{2,1,0:T(8,128)S(1)} %shard_map.58), channel_id=1, replica_groups=mesh['dp'=8,'fsdp'=8,'tensor'=8] {'fsdp'}, dimensions={0} | all-to-all | bytes 393216 | tf_op jit(solution)/shard_map/all_to_all | solution.py:186
  75.5 0.0 copy-start.1
  75.6 0.7 broadcast_in_dim.19
  76.2 3.4 %all-to-all-start.3 = ((f32[8,32,128]{2,1,0:T(8,128)}), f32[8,32,128]{2,1,0:T(8,128)S(1)}, u32[]{:S(2)}, u32[]{:S(2)}) async-start(f32[8,32,128]{2,1,0:T(8,128)} %broadcast_in_dim.19), calls=%async_computation.3 | async-start | bytes 262144 | tf_op jit(solution)/shard_map/all_to_all | solution.py:190
  79.6 0.0 copy-done.1
  79.6 0.0 slice-start
  79.6 7.8 %all-to-all-done.3 = f32[8,32,128]{2,1,0:T(8,128)S(1)} async-done(((f32[8,32,128]{2,1,0:T(8,128)}), f32[8,32,128]{2,1,0:T(8,128)S(1)}, u32[]{:S(2)}, u32[]{:S(2)}) %all-to-all-start.3) | async-done | bytes 131104 | tf_op jit(solution)/shard_map/all_to_all | solution.py:190
  87.5 0.0 slice-done
  87.5 10.7 %all_to_all.33.whole_ref = f32[8,48,128]{2,1,0:T(8,128)S(1)} all-to-all(f32[8,48,128]{2,1,0:T(8,128)S(1)} %broadcast_in_dim.20), channel_id=1, replica_groups=mesh['dp'=8,'fsdp'=8,'tensor'=8] {'fsdp'}, dimensions={0} | all-to-all | bytes 393216 | tf_op jit(solution)/shard_map/all_to_all | solution.py:190
  98.2 5.4 %shard_map.59 = (f32[128,128]{1,0:T(8,128)S(1)}, f32[256,128]{1,0:T(8,128)S(1)}, f32[8,1,128]{2,1,0:T(1,128)}) custom-call(f32[8,48,128]{2,1,0:T(8,128)S(1)} %all_to_all.33.whole_ref), custom_call_target="tpu_custom_call" | custom-call | tf_op jit(solution)/shard_map/pallas_call | solution.py:97
  103.6 0.5 fusion.4.left_ref
  104.1 3.3 %all-to-all-start.5 = ((f32[8,1,128]{2,1,0:T(1,128)}), f32[8,1,128]{2,1,0:T(1,128)S(1)}, u32[]{:S(2)}, u32[]{:S(2)}) async-start(f32[8,1,128]{2,1,0:T(1,128)} %get-tuple-element.10), calls=%async_computation.5 | async-start | bytes 8192 | tf_op jit(solution)/shard_map/all_to_all | solution.py:206
  107.5 1.8 %fusion.1 = f32[1,1,896,256]{3,2,1,0:T(8,128)} fusion(f32[896,256]{1,0:T(8,128)S(1)} %add_bitcast_fusion.blended_ref, f32[896,128]{1,0:T(8,128)S(1)} %fusion.4.left_ref, f32[256,128]{1,0:T(8,128)S(1)} %get-tuple-element.9.reduced_ref), kind=kOutput, calls=%fused_computation.2 | convolution fusion | flops 352780288 | bytes 2424832 | tf_op jit(solution)/shard_map/dot_general | solution.py:33
  109.3 4.6 %all-to-all-done.5.squares_ref = f32[8,1,128]{2,1,0:T(1,128)S(1)} async-done(((f32[8,1,128]{2,1,0:T(1,128)}), f32[8,1,128]{2,1,0:T(1,128)S(1)}, u32[]{:S(2)}, u32[]{:S(2)}) %all-to-all-start.5) | async-done | bytes 4128 | tf_op jit(solution)/shard_map/all_to_all | solution.py:206
  113.8 1.3 %shard_map.60 = (f32[256,128]{1,0:T(8,128)}, bf16[896,256]{1,0:T(8,128)(2,1)}) custom-call(f32[896,128]{1,0:T(8,128)S(1)} %fusion.4.left_ref, f32[256,128]{1,0:T(8,128)S(1)} %get-tuple-element.9.reduced_ref, f32[8,1,128]{2,1,0:T(1,128)S(1)} %all-to-all-done.5.squares_ref), custom_call_target="tpu_custom_call" | custom-call | tf_op jit(solution)/shard_map/pallas_call | solution.py:168
  (8 shorter events, 0.2 us)
Async XLA Ops:
  0.6 1.4 %copy-start = (f32[1,256,128]{2,1,0:T(8,128)S(1)}, f32[1,256,128]{2,1,0:T(8,128)}, u32[]{:S(2)}) copy-start(f32[1,256,128]{2,1,0:T(8,128)} %param.5) | copy-start | bytes 393220
  75.5 4.1 %copy-start.1 = (f32[48,128]{1,0:T(8,128)}, f32[48,128]{1,0:T(8,128)S(1)}, u32[]{:S(2)}) copy-start(f32[48,128]{1,0:T(8,128)S(1)} %reduce_sum.28) | copy-start | bytes 73732
  76.2 11.2 %all-to-all-start.3 = ((f32[8,32,128]{2,1,0:T(8,128)}), f32[8,32,128]{2,1,0:T(8,128)S(1)}, u32[]{:S(2)}, u32[]{:S(2)}) async-start(f32[8,32,128]{2,1,0:T(8,128)} %broadcast_in_dim.19), calls=%async_computation.3 | async-start | bytes 262144 | tf_op jit(solution)/shard_map/all_to_all | solution.py:190
  79.6 7.9 %slice-start = ((f32[48,128]{1,0:T(8,128)}), f32[16,128]{1,0:T(8,128)S(1)}, s32[]{:S(2)}) async-start(f32[48,128]{1,0:T(8,128)} %copy-done.1), calls=%async_computation.6 | async-start | bytes 16384 | tf_op jit(solution)/shard_map/slice | solution.py:204
  104.1 9.7 %all-to-all-start.5 = ((f32[8,1,128]{2,1,0:T(1,128)}), f32[8,1,128]{2,1,0:T(1,128)S(1)}, u32[]{:S(2)}, u32[]{:S(2)}) async-start(f32[8,1,128]{2,1,0:T(1,128)} %get-tuple-element.10), calls=%async_computation.5 | async-start | bytes 8192 | tf_op jit(solution)/shard_map/all_to_all | solution.py:206

commit v5 on v4

--- a/solution.py
+++ b/solution.py
@@ -137,24 +137,63 @@
     return high, (x - high.astype(jnp.float32)).astype(jnp.bfloat16)
 
 
+def outer_of_halves(left, right):
+    def outer(left, right):
+        return lax.dot_general(left, right, (((1,), (1,)), ((), ())), preferred_element_type=jnp.float32)
+
+    return outer(left[0], right[0]) + (outer(left[0], right[1]) + outer(left[1], right[0]))
+
+
+def moment_kernel(blended_ref, projected_ref, inverse_ref, reduced_ref, left_ref, moment_out, moment_ref, sems):
+    steps = sems.shape[0]
+    rows = left_ref.shape[0] // steps
+    inverse = inverse_ref[...]
+    right = halves(reduced_ref[...] * (1.0 - decay_rate))
+    copies = []
+    for step in range(steps):
+        block = pl.ds(step * rows, rows)
+        left = outer_cols(projected_ref[block, :], inverse)
+        left_ref[block, :] = left
+        moment_ref[block, :] = blended_ref[block, :] - outer_of_halves(halves(left), right)
+        copies.append(pltpu.make_async_copy(moment_ref.at[block], moment_out.at[block], sems.at[step]))
+        copies[-1].start()
+    for copy in copies:
+        copy.wait()
+
+
+def left_and_moment(blended, projected, inverse_low, reduced):
+    steps = 4
+    rows, cols = blended.shape
+    vmem, anywhere = pl.BlockSpec(memory_space=pltpu.VMEM), pl.BlockSpec(memory_space=pl.ANY)
+    return pl.pallas_call(
+        moment_kernel,
+        out_shape=(
+            jax.ShapeDtypeStruct((rows, RANK), jnp.float32),
+            jax.ShapeDtypeStruct((rows, cols), jnp.float32),
+        ),
+        in_specs=[vmem] * 4,
+        out_specs=[vmem, anywhere],
+        scratch_shapes=[pltpu.VMEM((rows, cols), jnp.float32), pltpu.SemaphoreType.DMA((steps,))],
+        compiler_params=pltpu.CompilerParams(vmem_limit_bytes=24 * 2**20),
+        cost_estimate=pl.CostEstimate(
+            flops=12 * rows * cols * RANK, bytes_accessed=4 * rows * cols, transcendentals=0
+        ),
+    )(blended, projected, inverse_low, reduced)
+
+
 def update_kernel(left_ref, reduced_ref, squares_ref, right_out, update_out, right_ref, update_ref, sems):
     steps = sems.shape[0] - 1
     rows = left_ref.shape[0] // steps
-
-    def outer(left, right):
-        return lax.dot_general(left, right, (((1,), (1,)), ((), ())), preferred_element_type=jnp.float32)
 
     norm = jnp.sqrt(jnp.sum(squares_ref[...], axis=0)) + epsilon
     right_new = reduced_ref[...] / norm
     right_ref[...] = right_new
     copies = [pltpu.make_async_copy(right_ref, right_out, sems.at[steps])]
     copies[0].start()
-    right_high, right_low = halves(right_new * math.sqrt(M_ROWS * N_COLS / RANK))
+    right = halves(right_new * math.sqrt(M_ROWS * N_COLS / RANK))
     for step in range(steps):
         block = pl.ds(step * rows, rows)
-        left_high, left_low = halves(left_ref[block, :])
-        total = outer(left_high, right_high) + (outer(left_high, right_low) + outer(left_low, right_high))
-        update_ref[block, :] = total.astype(jnp.bfloat16)
+        update_ref[block, :] = outer_of_halves(halves(left_ref[block, :]), right).astype(jnp.bfloat16)
         copies.append(pltpu.make_async_copy(update_ref.at[block], update_out.at[block], sems.at[step]))
         copies[-1].start()
     for copy in copies:
@@ -190,22 +229,27 @@
     return lax.all_to_all(jnp.broadcast_to(block, (count,) + block.shape), axes, 0, 0)
 
 
+def split_at(rows, where):
+    return rows[:where], rows[where:]
+
+
 def body(momentum, gradient, right_factor):
     n_dp, n_fsdp, n_tensor = (lax.axis_size(a) for a in ("dp", "fsdp", "tensor"))
     blended = momentum[0, 0] + gradient[0, 0].astype(jnp.float32)
     rows, cols = blended.shape
     plane = n_dp * n_tensor
     partial = lax.optimization_barrier(product(blended, right_factor[0]))
-    part = scatter_sum(partial.reshape(plane, rows // plane, RANK), ("dp", "tensor"))
-    projected = gather(part, ("dp", "tensor"), plane).reshape(rows, RANK)
+    part = scatter_sum(partial.reshape(plane, rows // plane, RANK), ("tensor", "dp"))
+    projected = gather(part, ("tensor", "dp"), plane).reshape(rows, RANK)
     own = cols // n_fsdp
-    held = scatter_sum(inner_products(blended, projected, n_fsdp), "fsdp")
-    summed = jnp.sum(gather(held[:own], "dp", n_dp), axis=0)
-    whole = gather(jnp.concatenate([summed, held[own:]], axis=0), "fsdp", n_fsdp)
+    right_raw, gram = lax.optimization_barrier(
+        split_at(scatter_sum(inner_products(blended, projected, n_fsdp), "fsdp"), own)
+    )
+    summed, gram = lax.optimization_barrier((jnp.sum(gather(right_raw, "dp", n_dp), axis=0), gram))
+    whole = gather(jnp.concatenate([summed, gram], axis=0), "fsdp", n_fsdp)
     inverse_low, reduced, squares = whiten_right(whole, n_tensor)
     squares = lax.all_to_all(squares, "tensor", 0, 0)
-    orthonormal = outer_cols(projected, inverse_low)
-    moment = blended - (1.0 - decay_rate) * outer_cols(orthonormal, reduced)
+    orthonormal, moment = left_and_moment(blended, projected, inverse_low, reduced)
     right_new, update = update_and_right(orthonormal, reduced, squares)
     return moment[None, None], right_new[None], update[None]
 

time: 116 us -> 115 us (level)
  blocking collectives: 81.9 us -> 93.4 us
  waiting for transfers between devices: 12.4 us -> 3.62 us
  starting transfers between devices: 6.69 us -> 3.31 us
  Pallas kernels: 7.81 us -> 10.6 us
  matrix products: 3.23 us -> 0.89 us
    all_to_all x2 -> x3, blocking collectives: 33.1 us -> 46 us  [gather(): lax.all_to_all(jnp.broadcast_to(block, (count,) + block.shape), axes, 0, 0)]
    all_to_all x1 -> x0, waiting for transfers between devices: 7.84 us -> none  [gather(): lax.all_to_all(jnp.broadcast_to(block, (count,) + block.shape), axes, 0, 0)]
    all_to_all x1 -> x0, starting transfers between devices: 3.37 us -> none  [gather(): lax.all_to_all(jnp.broadcast_to(block, (count,) + block.shape), axes, 0, 0)]
    pallas_call x0 -> x1, Pallas kernels: none -> 2.75 us  [left_and_moment(): pl.pallas_call(moment_kernel, out_shape=(jax.ShapeDtypeStruct((rows, RANK...]
    dot_general x2 -> x0, matrix products: 2.34 us -> none  [outer_cols(): lax.dot_general(left, right, (((1,), (1,)), ((), ())), precision=highest,...]
    all_to_all x2, blocking collectives: 48.7 us -> 47.3 us  [scatter_sum(): return jnp.sum(lax.all_to_all(blocks, axes, 0, 0), axis=0)]
  transfers between devices with their start and end apart: 2 -> 1, of which waited for: 2 -> 1; matrix products, arithmetic and copies ran while one was open for 2% -> 0% of each run, Pallas kernels for 0% -> 2%
where the time goes in v5:
time: 115 us; the launch traced here: 114 us
  blocking collectives  93.4 us (81%)
  Pallas kernels  10.6 us (9%)
  waiting for transfers between devices  3.62 us (3%)
  starting transfers between devices  3.31 us (3%)
  other arithmetic  1.53 us (1%)
    all_to_all x2, blocking collectives, scatter_sum(): return jnp.sum(lax.all_to_all(blocks, axes, 0, 0), axis=0)  47.3 us
    all_to_all x3, blocking collectives, gather(): lax.all_to_all(jnp.broadcast_to(block, (count,) + block.shape), axes, 0, 0)  46 us
    pallas_call x1, Pallas kernels, whiten_right(): pl.pallas_call(whiten_kernel, out_shape=(jax.ShapeDtypeStruct((RANK, RANK...  5.39 us
    all_to_all x1, waiting for transfers between devices, body(): squares = lax.all_to_all(squares, 'tensor', 0, 0)  3.62 us
    all_to_all x1, starting transfers between devices, body(): squares = lax.all_to_all(squares, 'tensor', 0, 0)  3.31 us
    pallas_call x1, Pallas kernels, left_and_moment(): pl.pallas_call(moment_kernel, out_shape=(jax.ShapeDtypeStruct((rows, RANK...  2.75 us
  transfers between devices with their start and end apart: 1, of which 1 were waited for; matrix products, arithmetic and copies ran while one was open for 0% of the time, Pallas kernels for 2%

profile of v5, /device:TPU:1, one launch (start us, length us, event | category | flops | bytes accessed | tf_op | source)
XLA Modules:
  0.0 114.2 jit_solution(14630576329583190558)
XLA Ops:
  0.6 0.0 copy-start
  0.6 1.4 %add_bitcast_fusion.blended_ref = f32[896,256]{1,0:T(8,128)S(1)} fusion(f32[1,1,896,256]{3,2,1,0:T(8,128)} %param.3, bf16[1,1,896,256]{3,2,1,0:T(8,128)(2,1)} %param.4), kind=kLoop, calls=%fused_computation | loop fusion | flops 458752 | bytes 2293760 | tf_op jit(solution)/shard_map/add | solution.py:238
  2.1 0.0 copy-done
  2.1 0.9 fusion
  3.0 33.3 %all_to_all.30 = f32[64,14,128]{2,1,0:T(8,128)S(1)} all-to-all(f32[64,14,128]{2,1,0:T(8,128)S(1)} %reshape.15), channel_id=1, replica_groups=mesh['dp'=8,'fsdp'=8,'tensor'=8] {'tensor','dp'}, dimensions={0} | all-to-all | bytes 917504 | tf_op jit(solution)/shard_map/all_to_all | solution.py:225
  36.3 0.1 reduce_sum.27
  36.4 23.7 %all_to_all.31 = f32[64,14,128]{2,1,0:T(8,128)S(1)} all-to-all(f32[64,14,128]{2,1,0:T(8,128)S(1)} %broadcast_in_dim.18), channel_id=1, replica_groups=mesh['dp'=8,'fsdp'=8,'tensor'=8] {'tensor','dp'}, dimensions={0} | all-to-all | bytes 917504 | tf_op jit(solution)/shard_map/all_to_all | solution.py:229
  60.2 1.1 shard_map.58
  61.3 14.1 %all_to_all.32 = f32[8,48,128]{2,1,0:T(8,128)S(1)} all-to-all(f32[8,48,128]{2,1,0:T(8,128)S(1)} %shard_map.58), channel_id=1, replica_groups=mesh['dp'=8,'fsdp'=8,'tensor'=8] {'fsdp'}, dimensions={0} | all-to-all | bytes 393216 | tf_op jit(solution)/shard_map/all_to_all | solution.py:225
  75.4 11.7 %all_to_all.33 = f32[8,32,128]{2,1,0:T(8,128)S(1)} all-to-all(f32[8,32,128]{2,1,0:T(8,128)S(1)} %broadcast_in_dim.19), channel_id=1, replica_groups=mesh['dp'=8,'fsdp'=8,'tensor'=8] {'dp'}, dimensions={0} | all-to-all | bytes 262144 | tf_op jit(solution)/shard_map/all_to_all | solution.py:229
  87.2 10.7 %all_to_all.34.whole_ref = f32[8,48,128]{2,1,0:T(8,128)S(1)} all-to-all(f32[8,48,128]{2,1,0:T(8,128)S(1)} %broadcast_in_dim.20), channel_id=1, replica_groups=mesh['dp'=8,'fsdp'=8,'tensor'=8] {'fsdp'}, dimensions={0} | all-to-all | bytes 393216 | tf_op jit(solution)/shard_map/all_to_all | solution.py:229
  97.8 5.4 %shard_map.59 = (f32[128,128]{1,0:T(8,128)S(1)}, f32[256,128]{1,0:T(8,128)S(1)}, f32[8,1,128]{2,1,0:T(1,128)}) custom-call(f32[8,48,128]{2,1,0:T(8,128)S(1)} %all_to_all.34.whole_ref), custom_call_target="tpu_custom_call" | custom-call | tf_op jit(solution)/shard_map/pallas_call | solution.py:97
  103.2 3.3 %all-to-all-start.5 = ((f32[8,1,128]{2,1,0:T(1,128)}), f32[8,1,128]{2,1,0:T(1,128)S(1)}, u32[]{:S(2)}, u32[]{:S(2)}) async-start(f32[8,1,128]{2,1,0:T(1,128)} %get-tuple-element.22), calls=%async_computation.5 | async-start | bytes 8192 | tf_op jit(solution)/shard_map/all_to_all | solution.py:251
  106.5 2.7 %shard_map.60 = (f32[896,128]{1,0:T(8,128)S(1)}, f32[896,256]{1,0:T(8,128)}) custom-call(f32[896,256]{1,0:T(8,128)S(1)} %add_bitcast_fusion.blended_ref, f32[896,128]{1,0:T(8,128)S(1)} %reshape.16.projected_ref, f32[128,128]{1,0:T(8,128)S(1)} %get-tuple-element.18.inverse_ref, f32[256,128]{1,0:T(8,128)S(1)} %get-tuple-element.19.reduced_ref), custom_call_target="tpu_custom_call" | custom-call | flops 352321536 | bytes 917504 | tf_op jit(solution)/shard_map/pallas_call | solution.py:168
  109.3 3.6 %all-to-all-done.5.squares_ref = f32[8,1,128]{2,1,0:T(1,128)S(1)} async-done(((f32[8,1,128]{2,1,0:T(1,128)}), f32[8,1,128]{2,1,0:T(1,128)S(1)}, u32[]{:S(2)}, u32[]{:S(2)}) %all-to-all-start.5) | async-done | bytes 4128 | tf_op jit(solution)/shard_map/all_to_all | solution.py:251
  112.9 1.3 %shard_map.61 = (f32[256,128]{1,0:T(8,128)}, bf16[896,256]{1,0:T(8,128)(2,1)}) custom-call(f32[896,128]{1,0:T(8,128)S(1)} %get-tuple-element.21.left_ref, f32[256,128]{1,0:T(8,128)S(1)} %get-tuple-element.19.reduced_ref, f32[8,1,128]{2,1,0:T(1,128)S(1)} %all-to-all-done.5.squares_ref), custom_call_target="tpu_custom_call" | custom-call | tf_op jit(solution)/shard_map/pallas_call | solution.py:207
  (10 shorter events, 0.2 us)
Async XLA Ops:
  0.6 1.4 %copy-start = (f32[1,256,128]{2,1,0:T(8,128)S(1)}, f32[1,256,128]{2,1,0:T(8,128)}, u32[]{:S(2)}) copy-start(f32[1,256,128]{2,1,0:T(8,128)} %param.5) | copy-start | bytes 393220
  103.2 9.7 %all-to-all-start.5 = ((f32[8,1,128]{2,1,0:T(1,128)}), f32[8,1,128]{2,1,0:T(1,128)S(1)}, u32[]{:S(2)}, u32[]{:S(2)}) async-start(f32[8,1,128]{2,1,0:T(1,128)} %get-tuple-element.22), calls=%async_computation.5 | async-start | bytes 8192 | tf_op jit(solution)/shard_map/all_to_all | solution.py:251

commit v6 on v5

--- a/solution.py
+++ b/solution.py
@@ -229,24 +229,25 @@
     return lax.all_to_all(jnp.broadcast_to(block, (count,) + block.shape), axes, 0, 0)
 
 
-def split_at(rows, where):
-    return rows[:where], rows[where:]
-
-
 def body(momentum, gradient, right_factor):
-    n_dp, n_fsdp, n_tensor = (lax.axis_size(a) for a in ("dp", "fsdp", "tensor"))
+    n_far, n_near, n_fsdp, n_tensor = (lax.axis_size(a) for a in ("dp_far", "dp_near", "fsdp", "tensor"))
     blended = momentum[0, 0] + gradient[0, 0].astype(jnp.float32)
     rows, cols = blended.shape
-    plane = n_dp * n_tensor
+    plane = ("dp_far", "dp_near", "tensor")
+    count = n_far * n_near * n_tensor
+    blocks, lines = (count, rows // count, RANK), (count, 1, rows // count * RANK)
     partial = lax.optimization_barrier(product(blended, right_factor[0]))
-    part = scatter_sum(partial.reshape(plane, rows // plane, RANK), ("tensor", "dp"))
-    projected = gather(part, ("tensor", "dp"), plane).reshape(rows, RANK)
-    own = cols // n_fsdp
-    right_raw, gram = lax.optimization_barrier(
-        split_at(scatter_sum(inner_products(blended, projected, n_fsdp), "fsdp"), own)
-    )
-    summed, gram = lax.optimization_barrier((jnp.sum(gather(right_raw, "dp", n_dp), axis=0), gram))
-    whole = gather(jnp.concatenate([summed, gram], axis=0), "fsdp", n_fsdp)
+    parts = lax.all_to_all(partial.reshape(lines), plane, 0, 0).reshape(rows, RANK)
+    part = jnp.sum(lax.optimization_barrier(parts).reshape(blocks), axis=0)
+    copies = lax.optimization_barrier(jnp.broadcast_to(part, blocks).reshape(rows, RANK))
+    projected = lax.all_to_all(copies.reshape(lines), plane, 0, 0).reshape(rows, RANK)
+    group = ("fsdp", "dp_near")
+    count = n_fsdp * n_near
+    own = cols // count
+    held = scatter_sum(inner_products(blended, projected, count), group)
+    right_raw, gram = lax.optimization_barrier((held[:own], held[own:] * (1.0 / n_near)))
+    summed, gram = lax.optimization_barrier((jnp.sum(gather(right_raw, "dp_far", n_far), axis=0), gram))
+    whole = gather(jnp.concatenate([summed, gram], axis=0), group, count)
     inverse_low, reduced, squares = whiten_right(whole, n_tensor)
     squares = lax.all_to_all(squares, "tensor", 0, 0)
     orthonormal, moment = left_and_moment(blended, projected, inverse_low, reduced)
@@ -255,13 +256,18 @@
 
 
 def solution(mesh):
+    near = 2
+    n_dp, n_fsdp, n_tensor = (mesh.shape[a] for a in ("dp", "fsdp", "tensor"))
+    devices = mesh.devices.reshape(n_dp // near, near, n_fsdp, n_tensor)
+    mesh = jax.sharding.Mesh(devices, ("dp_far", "dp_near", "fsdp", "tensor"))
+    dp = ("dp_far", "dp_near")
     in_specs = (
-        P("dp", None, "fsdp", "tensor"),
-        P("dp", None, "fsdp", "tensor"),
+        P(dp, None, "fsdp", "tensor"),
+        P(dp, None, "fsdp", "tensor"),
         P(None, "tensor", None),
     )
     out_specs = (
-        P("dp", None, "fsdp", "tensor"),
+        P(dp, None, "fsdp", "tensor"),
         P(None, "tensor", None),
         P(None, "fsdp", "tensor"),
     )

time: 115 us -> 111 us (0.965)
  blocking collectives: 93.4 us -> 90.4 us
    all_to_all x0 -> x2, blocking collectives: none -> 54 us  [the longest x1 33.1 us: body(): lax.all_to_all(partial.reshape(lines), plane, 0, 0).reshape(rows, RANK)]
    all_to_all x2 -> x1, blocking collectives: 47.3 us -> 15.5 us  [scatter_sum(): return jnp.sum(lax.all_to_all(blocks, axes, 0, 0), axis=0)]
    all_to_all x3 -> x2, blocking collectives: 46 us -> 20.9 us  [gather(): lax.all_to_all(jnp.broadcast_to(block, (count,) + block.shape), axes, 0, 0)]
where the time goes in v6:
time: 111 us
  blocking collectives  90.4 us (81%)
  Pallas kernels  10.5 us (9%)
  waiting for transfers between devices  3.62 us (3%)
  starting transfers between devices  3.31 us (3%)
  other arithmetic  1.54 us (1%)
    all_to_all x1, blocking collectives, body(): lax.all_to_all(partial.reshape(lines), plane, 0, 0).reshape(rows, RANK)  33.1 us
    all_to_all x1, blocking collectives, body(): lax.all_to_all(copies.reshape(lines), plane, 0, 0).reshape(rows, RANK)  20.9 us
    all_to_all x2, blocking collectives, gather(): lax.all_to_all(jnp.broadcast_to(block, (count,) + block.shape), axes, 0, 0)  20.9 us
    all_to_all x1, blocking collectives, scatter_sum(): return jnp.sum(lax.all_to_all(blocks, axes, 0, 0), axis=0)  15.5 us
    pallas_call x1, Pallas kernels, whiten_right(): pl.pallas_call(whiten_kernel, out_shape=(jax.ShapeDtypeStruct((RANK, RANK...  5.39 us
    all_to_all x1, waiting for transfers between devices, body(): squares = lax.all_to_all(squares, 'tensor', 0, 0)  3.62 us
    all_to_all x1, starting transfers between devices, body(): squares = lax.all_to_all(squares, 'tensor', 0, 0)  3.31 us
    pallas_call x1, Pallas kernels, left_and_moment(): pl.pallas_call(moment_kernel, out_shape=(jax.ShapeDtypeStruct((rows, RANK...  2.75 us
  transfers between devices with their start and end apart: 1, of which 1 were waited for; matrix products, arithmetic and copies ran while one was open for 0% of the time, Pallas kernels for 2%

profile of v6, /device:TPU:1, one launch (start us, length us, event | category | flops | bytes accessed | tf_op | source)
XLA Modules:
  0.0 111.1 jit_solution(2784990183361496788)
XLA Ops:
  0.6 0.0 copy-start
  0.6 1.4 %add_bitcast_fusion.blended_ref = f32[896,256]{1,0:T(8,128)S(1)} fusion(f32[1,1,896,256]{3,2,1,0:T(8,128)} %param.3, bf16[1,1,896,256]{3,2,1,0:T(8,128)(2,1)} %param.4), kind=kLoop, calls=%fused_computation | loop fusion | flops 458752 | bytes 2293760 | tf_op jit(solution)/shard_map/add | solution.py:234
  2.1 0.0 copy-done
  2.1 0.9 fusion
  3.0 33.1 %all_to_all.30 = f32[64,1,1792]{2,1,0:T(1,128)S(1)} all-to-all(f32[64,1,1792]{2,1,0:T(1,128)S(1)} %bitcast.17), channel_id=1, replica_groups=mesh['dp_far'=4,'dp_near'=2,'fsdp'=8,'tensor'=8] {'dp_far','dp_near','te..., dimensions={0} | all-to-all | bytes 917504 | tf_op jit(solution)/shard_map/all_to_all | solution.py:240
  36.1 0.1 reduce_sum.27
  36.3 20.9 %all_to_all.31 = f32[64,1,1792]{2,1,0:T(1,128)S(1)} all-to-all(f32[64,1,1792]{2,1,0:T(1,128)S(1)} %bitcast.16), channel_id=1, replica_groups=mesh['dp_far'=4,'dp_near'=2,'fsdp'=8,'tensor'=8] {'dp_far','dp_near','te..., dimensions={0} | all-to-all | bytes 917504 | tf_op jit(solution)/shard_map/all_to_all | solution.py:243
  57.2 1.1 %shard_map.58 = f32[16,24,128]{2,1,0:T(8,128)S(1)} custom-call(f32[896,256]{1,0:T(8,128)S(1)} %add_bitcast_fusion.blended_ref, f32[896,128]{1,0:T(8,128)S(1)} %bitcast.13), custom_call_target="tpu_custom_call" | custom-call | tf_op jit(solution)/shard_map/pallas_call | solution.py:126
  58.3 15.5 %all_to_all.32 = f32[16,24,128]{2,1,0:T(8,128)S(1)} all-to-all(f32[16,24,128]{2,1,0:T(8,128)S(1)} %shard_map.58), channel_id=1, replica_groups=mesh['dp_far'=4,'dp_near'=2,'fsdp'=8,'tensor'=8] {'fsdp','dp_near'}, dimensions={0} | all-to-all | bytes 393216 | tf_op jit(solution)/shard_map/all_to_all | solution.py:225
  73.9 9.6 %all_to_all.33 = f32[4,16,128]{2,1,0:T(8,128)S(1)} all-to-all(f32[4,16,128]{2,1,0:T(8,128)S(1)} %broadcast_in_dim.19), channel_id=1, replica_groups=mesh['dp_far'=4,'dp_near'=2,'fsdp'=8,'tensor'=8] {'dp_far'}, dimensions={0} | all-to-all | bytes 65536 | tf_op jit(solution)/shard_map/all_to_all | solution.py:229
  83.5 11.3 %all_to_all.34.whole_ref = f32[16,24,128]{2,1,0:T(8,128)S(1)} all-to-all(f32[16,24,128]{2,1,0:T(8,128)S(1)} %broadcast_in_dim.20), channel_id=1, replica_groups=mesh['dp_far'=4,'dp_near'=2,'fsdp'=8,'tensor'=8] {'fsdp','dp_near'}, dimensions={0} | all-to-all | bytes 393216 | tf_op jit(solution)/shard_map/all_to_all | solution.py:229
  94.8 5.4 %shard_map.59 = (f32[128,128]{1,0:T(8,128)S(1)}, f32[256,128]{1,0:T(8,128)S(1)}, f32[8,1,128]{2,1,0:T(1,128)}) custom-call(f32[16,24,128]{2,1,0:T(8,128)S(1)} %all_to_all.34.whole_ref), custom_call_target="tpu_custom_call" | custom-call | tf_op jit(solution)/shard_map/pallas_call | solution.py:97
  100.2 3.3 %all-to-all-start.5 = ((f32[8,1,128]{2,1,0:T(1,128)}), f32[8,1,128]{2,1,0:T(1,128)S(1)}, u32[]{:S(2)}, u32[]{:S(2)}) async-start(f32[8,1,128]{2,1,0:T(1,128)} %get-tuple-element.22), calls=%async_computation.5 | async-start | bytes 8192 | tf_op jit(solution)/shard_map/all_to_all | solution.py:252
  103.5 2.7 %shard_map.60 = (f32[896,128]{1,0:T(8,128)S(1)}, f32[896,256]{1,0:T(8,128)}) custom-call(f32[896,256]{1,0:T(8,128)S(1)} %add_bitcast_fusion.blended_ref, f32[896,128]{1,0:T(8,128)S(1)} %bitcast.14, f32[128,128]{1,0:T(8,128)S(1)} %get-tuple-element.18.inverse_ref, f32[256,128]{1,0:T(8,128)S(1)} %get-tuple-element.19.reduced_ref), custom_call_target="tpu_custom_call" | custom-call | flops 352321536 | bytes 917504 | tf_op jit(solution)/shard_map/pallas_call | solution.py:168
  106.2 3.6 %all-to-all-done.5.squares_ref = f32[8,1,128]{2,1,0:T(1,128)S(1)} async-done(((f32[8,1,128]{2,1,0:T(1,128)}), f32[8,1,128]{2,1,0:T(1,128)S(1)}, u32[]{:S(2)}, u32[]{:S(2)}) %all-to-all-start.5) | async-done | bytes 4128 | tf_op jit(solution)/shard_map/all_to_all | solution.py:252
  109.9 1.3 %shard_map.61 = (f32[256,128]{1,0:T(8,128)}, bf16[896,256]{1,0:T(8,128)(2,1)}) custom-call(f32[896,128]{1,0:T(8,128)S(1)} %get-tuple-element.21.left_ref, f32[256,128]{1,0:T(8,128)S(1)} %get-tuple-element.19.reduced_ref, f32[8,1,128]{2,1,0:T(1,128)S(1)} %all-to-all-done.5.squares_ref), custom_call_target="tpu_custom_call" | custom-call | tf_op jit(solution)/shard_map/pallas_call | solution.py:207
  (10 shorter events, 0.2 us)
Async XLA Ops:
  0.6 1.4 %copy-start = (f32[1,256,128]{2,1,0:T(8,128)S(1)}, f32[1,256,128]{2,1,0:T(8,128)}, u32[]{:S(2)}) copy-start(f32[1,256,128]{2,1,0:T(8,128)} %param.5) | copy-start | bytes 393220
  100.2 9.7 %all-to-all-start.5 = ((f32[8,1,128]{2,1,0:T(1,128)}), f32[8,1,128]{2,1,0:T(1,128)S(1)}, u32[]{:S(2)}, u32[]{:S(2)}) async-start(f32[8,1,128]{2,1,0:T(1,128)} %get-tuple-element.22), calls=%async_computation.5 | async-start | bytes 8192 | tf_op jit(solution)/shard_map/all_to_all | solution.py:252

commit v7 on v6

--- a/solution.py
+++ b/solution.py
@@ -12,6 +12,7 @@
 RANK = 128
 SUB = 8
 REPLICAS = 8
+DP = ("dp_4", "dp_2", "dp_1")
 
 
 highest = lax.Precision.HIGHEST
@@ -230,23 +231,23 @@
 
 
 def body(momentum, gradient, right_factor):
-    n_far, n_near, n_fsdp, n_tensor = (lax.axis_size(a) for a in ("dp_far", "dp_near", "fsdp", "tensor"))
+    n_dp, n_near, n_fsdp, n_tensor = (lax.axis_size(a) for a in (DP, "dp_1", "fsdp", "tensor"))
     blended = momentum[0, 0] + gradient[0, 0].astype(jnp.float32)
     rows, cols = blended.shape
-    plane = ("dp_far", "dp_near", "tensor")
-    count = n_far * n_near * n_tensor
+    plane = ("tensor", "dp_1", "dp_2", "dp_4")
+    count = n_dp * n_tensor
     blocks, lines = (count, rows // count, RANK), (count, 1, rows // count * RANK)
     partial = lax.optimization_barrier(product(blended, right_factor[0]))
     parts = lax.all_to_all(partial.reshape(lines), plane, 0, 0).reshape(rows, RANK)
     part = jnp.sum(lax.optimization_barrier(parts).reshape(blocks), axis=0)
     copies = lax.optimization_barrier(jnp.broadcast_to(part, blocks).reshape(rows, RANK))
     projected = lax.all_to_all(copies.reshape(lines), plane, 0, 0).reshape(rows, RANK)
-    group = ("fsdp", "dp_near")
+    group, far = ("dp_1", "fsdp"), ("dp_2", "dp_4")
     count = n_fsdp * n_near
     own = cols // count
     held = scatter_sum(inner_products(blended, projected, count), group)
     right_raw, gram = lax.optimization_barrier((held[:own], held[own:] * (1.0 / n_near)))
-    summed, gram = lax.optimization_barrier((jnp.sum(gather(right_raw, "dp_far", n_far), axis=0), gram))
+    summed, gram = lax.optimization_barrier((jnp.sum(gather(right_raw, far, n_dp // n_near), axis=0), gram))
     whole = gather(jnp.concatenate([summed, gram], axis=0), group, count)
     inverse_low, reduced, squares = whiten_right(whole, n_tensor)
     squares = lax.all_to_all(squares, "tensor", 0, 0)
@@ -256,18 +257,16 @@
 
 
 def solution(mesh):
-    near = 2
     n_dp, n_fsdp, n_tensor = (mesh.shape[a] for a in ("dp", "fsdp", "tensor"))
-    devices = mesh.devices.reshape(n_dp // near, near, n_fsdp, n_tensor)
-    mesh = jax.sharding.Mesh(devices, ("dp_far", "dp_near", "fsdp", "tensor"))
-    dp = ("dp_far", "dp_near")
+    devices = mesh.devices.reshape(n_dp // 4, 2, 2, n_fsdp, n_tensor)
+    mesh = jax.sharding.Mesh(devices, DP + ("fsdp", "tensor"))
     in_specs = (
-        P(dp, None, "fsdp", "tensor"),
-        P(dp, None, "fsdp", "tensor"),
+        P(DP, None, "fsdp", "tensor"),
+        P(DP, None, "fsdp", "tensor"),
         P(None, "tensor", None),
     )
     out_specs = (
-        P(dp, None, "fsdp", "tensor"),
+        P(DP, None, "fsdp", "tensor"),
         P(None, "tensor", None),
         P(None, "fsdp", "tensor"),
     )

time: 111 us -> 112 us (level)
    all_to_all x1, blocking collectives: 33.1 us -> 34.7 us  [body(): lax.all_to_all(partial.reshape(lines), plane, 0, 0).reshape(rows, RANK)]
where the time goes in v7:
time: 112 us
  blocking collectives  91.1 us (81%)
  Pallas kernels  10.6 us (9%)
  waiting for transfers between devices  3.62 us (3%)
  starting transfers between devices  3.31 us (3%)
  other arithmetic  1.54 us (1%)
    all_to_all x1, blocking collectives, body(): lax.all_to_all(partial.reshape(lines), plane, 0, 0).reshape(rows, RANK)  34.7 us
    all_to_all x1, blocking collectives, body(): lax.all_to_all(copies.reshape(lines), plane, 0, 0).reshape(rows, RANK)  21 us
    all_to_all x2, blocking collectives, gather(): lax.all_to_all(jnp.broadcast_to(block, (count,) + block.shape), axes, 0, 0)  20.1 us
    all_to_all x1, blocking collectives, scatter_sum(): return jnp.sum(lax.all_to_all(blocks, axes, 0, 0), axis=0)  15.3 us
    pallas_call x1, Pallas kernels, whiten_right(): pl.pallas_call(whiten_kernel, out_shape=(jax.ShapeDtypeStruct((RANK, RANK...  5.39 us
    all_to_all x1, waiting for transfers between devices, body(): squares = lax.all_to_all(squares, 'tensor', 0, 0)  3.62 us
    all_to_all x1, starting transfers between devices, body(): squares = lax.all_to_all(squares, 'tensor', 0, 0)  3.31 us
    pallas_call x1, Pallas kernels, left_and_moment(): pl.pallas_call(moment_kernel, out_shape=(jax.ShapeDtypeStruct((rows, RANK...  2.75 us
  transfers between devices with their start and end apart: 1, of which 1 were waited for; matrix products, arithmetic and copies ran while one was open for 0% of the time, Pallas kernels for 2%

profile of v7, /device:TPU:1, one launch (start us, length us, event | category | flops | bytes accessed | tf_op | source)
XLA Modules:
  0.0 111.8 jit_solution(10788796937934841235)
XLA Ops:
  0.6 0.0 copy-start
  0.6 1.4 %add_bitcast_fusion.blended_ref = f32[896,256]{1,0:T(8,128)S(1)} fusion(f32[1,1,896,256]{3,2,1,0:T(8,128)} %param.3, bf16[1,1,896,256]{3,2,1,0:T(8,128)(2,1)} %param.4), kind=kLoop, calls=%fused_computation | loop fusion | flops 458752 | bytes 2293760 | tf_op jit(solution)/shard_map/add | solution.py:235
  2.1 0.0 copy-done
  2.1 0.9 fusion
  3.0 34.7 %all_to_all.30 = f32[64,1,1792]{2,1,0:T(1,128)S(1)} all-to-all(f32[64,1,1792]{2,1,0:T(1,128)S(1)} %bitcast.17), channel_id=1, replica_groups=mesh['dp_4'=2,'dp_2'=2,'dp_1'=2,'fsdp'=8,'tensor'=8] {'tensor','dp_1','d..., dimensions={0} | all-to-all | bytes 917504 | tf_op jit(solution)/shard_map/all_to_all | solution.py:241
  37.7 0.1 reduce_sum.27
  37.8 21.0 %all_to_all.31 = f32[64,1,1792]{2,1,0:T(1,128)S(1)} all-to-all(f32[64,1,1792]{2,1,0:T(1,128)S(1)} %bitcast.16), channel_id=1, replica_groups=mesh['dp_4'=2,'dp_2'=2,'dp_1'=2,'fsdp'=8,'tensor'=8] {'tensor','dp_1','d..., dimensions={0} | all-to-all | bytes 917504 | tf_op jit(solution)/shard_map/all_to_all | solution.py:244
  58.9 1.1 %shard_map.58 = f32[16,24,128]{2,1,0:T(8,128)S(1)} custom-call(f32[896,256]{1,0:T(8,128)S(1)} %add_bitcast_fusion.blended_ref, f32[896,128]{1,0:T(8,128)S(1)} %bitcast.13), custom_call_target="tpu_custom_call" | custom-call | tf_op jit(solution)/shard_map/pallas_call | solution.py:127
  60.0 15.3 %all_to_all.32 = f32[16,24,128]{2,1,0:T(8,128)S(1)} all-to-all(f32[16,24,128]{2,1,0:T(8,128)S(1)} %shard_map.58), channel_id=1, replica_groups=mesh['dp_4'=2,'dp_2'=2,'dp_1'=2,'fsdp'=8,'tensor'=8] {'dp_1','fsdp'}, dimensions={0} | all-to-all | bytes 393216 | tf_op jit(solution)/shard_map/all_to_all | solution.py:226
  75.4 9.0 %all_to_all.33 = f32[4,16,128]{2,1,0:T(8,128)S(1)} all-to-all(f32[4,16,128]{2,1,0:T(8,128)S(1)} %broadcast_in_dim.19), channel_id=1, replica_groups=mesh['dp_4'=2,'dp_2'=2,'dp_1'=2,'fsdp'=8,'tensor'=8] {'dp_2','dp_4'}, dimensions={0} | all-to-all | bytes 65536 | tf_op jit(solution)/shard_map/all_to_all | solution.py:230
  84.4 11.1 %all_to_all.34.whole_ref = f32[16,24,128]{2,1,0:T(8,128)S(1)} all-to-all(f32[16,24,128]{2,1,0:T(8,128)S(1)} %broadcast_in_dim.20), channel_id=1, replica_groups=mesh['dp_4'=2,'dp_2'=2,'dp_1'=2,'fsdp'=8,'tensor'=8] {'dp_1','fsdp'}, dimensions={0} | all-to-all | bytes 393216 | tf_op jit(solution)/shard_map/all_to_all | solution.py:230
  95.5 5.4 %shard_map.59 = (f32[128,128]{1,0:T(8,128)S(1)}, f32[256,128]{1,0:T(8,128)S(1)}, f32[8,1,128]{2,1,0:T(1,128)}) custom-call(f32[16,24,128]{2,1,0:T(8,128)S(1)} %all_to_all.34.whole_ref), custom_call_target="tpu_custom_call" | custom-call | tf_op jit(solution)/shard_map/pallas_call | solution.py:98
  100.9 3.3 %all-to-all-start.5 = ((f32[8,1,128]{2,1,0:T(1,128)}), f32[8,1,128]{2,1,0:T(1,128)S(1)}, u32[]{:S(2)}, u32[]{:S(2)}) async-start(f32[8,1,128]{2,1,0:T(1,128)} %get-tuple-element.22), calls=%async_computation.5 | async-start | bytes 8192 | tf_op jit(solution)/shard_map/all_to_all | solution.py:253
  104.2 2.7 %shard_map.60 = (f32[896,128]{1,0:T(8,128)S(1)}, f32[896,256]{1,0:T(8,128)}) custom-call(f32[896,256]{1,0:T(8,128)S(1)} %add_bitcast_fusion.blended_ref, f32[896,128]{1,0:T(8,128)S(1)} %bitcast.14, f32[128,128]{1,0:T(8,128)S(1)} %get-tuple-element.18.inverse_ref, f32[256,128]{1,0:T(8,128)S(1)} %get-tuple-element.19.reduced_ref), custom_call_target="tpu_custom_call" | custom-call | flops 352321536 | bytes 917504 | tf_op jit(solution)/shard_map/pallas_call | solution.py:169
  106.9 3.6 %all-to-all-done.5.squares_ref = f32[8,1,128]{2,1,0:T(1,128)S(1)} async-done(((f32[8,1,128]{2,1,0:T(1,128)}), f32[8,1,128]{2,1,0:T(1,128)S(1)}, u32[]{:S(2)}, u32[]{:S(2)}) %all-to-all-start.5) | async-done | bytes 4128 | tf_op jit(solution)/shard_map/all_to_all | solution.py:253
  110.6 1.3 %shard_map.61 = (f32[256,128]{1,0:T(8,128)}, bf16[896,256]{1,0:T(8,128)(2,1)}) custom-call(f32[896,128]{1,0:T(8,128)S(1)} %get-tuple-element.21.left_ref, f32[256,128]{1,0:T(8,128)S(1)} %get-tuple-element.19.reduced_ref, f32[8,1,128]{2,1,0:T(1,128)S(1)} %all-to-all-done.5.squares_ref), custom_call_target="tpu_custom_call" | custom-call | tf_op jit(solution)/shard_map/pallas_call | solution.py:208
  (10 shorter events, 0.2 us)
Async XLA Ops:
  0.6 1.4 %copy-start = (f32[1,256,128]{2,1,0:T(8,128)S(1)}, f32[1,256,128]{2,1,0:T(8,128)}, u32[]{:S(2)}) copy-start(f32[1,256,128]{2,1,0:T(8,128)} %param.5) | copy-start | bytes 393220
  100.9 9.7 %all-to-all-start.5 = ((f32[8,1,128]{2,1,0:T(1,128)}), f32[8,1,128]{2,1,0:T(1,128)S(1)}, u32[]{:S(2)}, u32[]{:S(2)}) async-start(f32[8,1,128]{2,1,0:T(1,128)} %get-tuple-element.22), calls=%async_computation.5 | async-start | bytes 8192 | tf_op jit(solution)/shard_map/all_to_all | solution.py:253

commit v8 on v6

--- a/solution.py
+++ b/solution.py
@@ -35,29 +35,50 @@
     )
 
 
-def spread(row, count=SUB):
-    return jnp.broadcast_to(row, (count, RANK))
+def terms(x):
+    out = []
+    for _ in range(3):
+        out.append(x.astype(jnp.bfloat16))
+        x = x - out[-1].astype(jnp.float32)
+    return out
+
+
+def dot(left, right):
+    return jnp.dot(left, right, preferred_element_type=jnp.float32)
+
+
+def spread(row):
+    return jnp.broadcast_to(row, (SUB, RANK))
+
+
+def far_product(left, right):
+    l1, l2, l3 = terms(left)
+    r1, r2, r3 = terms(right)
+    return dot(jnp.concatenate([l1, l1, l2, l1, l3, l2], axis=1), jnp.concatenate([r1, r2, r1, r3, r1, r2], axis=0))
+
 
 def invert_factor(tiles, write):
     lane = lax.broadcasted_iota(jnp.int32, (SUB, RANK), 1)
+    sub = lax.broadcasted_iota(jnp.int32, (SUB, RANK), 0)
     count = len(tiles)
     for b in range(count):
         first = b * SUB
         panel = (lane >= first) & (lane < first + SUB)
-        below = range(b, count)
-        columns = {t: [jnp.broadcast_to(tiles[t][:, first + k:first + k + 1], (SUB, RANK)) for k in range(SUB)] for t in below}
+        near, far = range(b, min(b + 3, count)), range(b + 3, count)
+        columns = {
+            t: [jnp.broadcast_to(tiles[t][:, first + k:first + k + 1], (SUB, RANK)) for k in range(SUB)] for t in near
+        }
         pivot = [[spread(columns[b][j][k:k + 1]) if k >= j else None for k in range(SUB)] for j in range(SUB)]
         rows = [jnp.where(panel, (lane == first + p).astype(jnp.float32), spread(tiles[b][p:p + 1])) for p in range(SUB)]
         inverse = []
-        ratio = {}
         for j in range(SUB):
             inverse.append(1.0 / pivot[j][j])
             for i in range(j + 1, SUB):
-                ratio[i, j] = pivot[j][i] * inverse[j]
+                ratio = pivot[j][i] * inverse[j]
                 for k in range(i, SUB):
-                    pivot[i][k] = pivot[i][k] - ratio[i, j] * pivot[j][k]
-                rows[i] = rows[i] - ratio[i, j] * rows[j]
-        for t in range(b + 1, count):
+                    pivot[i][k] = pivot[i][k] - ratio * pivot[j][k]
+                rows[i] = rows[i] - ratio * rows[j]
+        for t in near[1:]:
             held = jnp.where(panel, 0.0, tiles[t])
             left = columns[t]
             for j in range(SUB):
@@ -66,11 +87,27 @@
                     left[k] = left[k] - multiple * pivot[j][k]
                 held = held - multiple * rows[j]
             tiles[t] = held
+        if far:
+            back = [None] * SUB
+            for j in reversed(range(SUB)):
+                row = rows[j]
+                for k in range(j + 1, SUB):
+                    row = row - pivot[j][k] * back[k]
+                back[j] = row * inverse[j]
+            block = back[0]
+            for p in range(1, SUB):
+                block = jnp.where(sub == p, back[p], block)
+            zero = jnp.zeros((SUB, RANK), jnp.float32)
+            block = jnp.concatenate([zero] * b + [block] + [zero] * (count - 1 - b), axis=0)
+            taken = far_product(jnp.concatenate([tiles[t] for t in far], axis=0), block)
+            for place, t in enumerate(far):
+                tiles[t] = jnp.where(panel, 0.0, tiles[t]) - taken[place * SUB:(place + 1) * SUB]
         for p in range(SUB):
             d = pivot[p][p]
             root = lax.rsqrt(d)
             root = root * (1.5 - 0.5 * d * root * root)
             write(first + p, jnp.where(lane <= first + p, rows[p] * root, 0.0)[0:1])
+
 
 def whiten_kernel(whole_ref, inverse_ref, reduced_ref, squares_ref):
     count, high, _ = whole_ref.shape
@@ -108,16 +145,19 @@
 
 
 def inner_kernel(blended_ref, projected_ref, out_ref):
-    count, high, _ = out_ref.shape
-    share = RANK // count
-    own = high - share
+    count, share = out_ref.shape[0], RANK // out_ref.shape[0]
+    own = out_ref.shape[1] - share
+    cols = count * own
     projected = projected_ref[...]
-    flipped = projected.T
-    right_raw = product(flipped, blended_ref[...]).T
-    gram = product(flipped, projected)
+    r1, r2, r3 = terms(projected)
+    l1, l2, l3 = terms(jnp.concatenate([blended_ref[...], projected], axis=1).T)
+    pair = jnp.concatenate([r1, r2], axis=1)
+    high, low = dot(l1, pair), dot(l2, pair)
+    rest = low[:, RANK:] + (dot(l1, r3) + dot(l3, r1))
+    both = high[:, :RANK] + ((high[:, RANK:] + low[:, :RANK]) + rest)
     for k in range(count):
-        out_ref[k, :own] = right_raw[k * own:(k + 1) * own]
-        out_ref[k, own:] = gram[k * share:(k + 1) * share]
+        out_ref[k, :own] = both[k * own:(k + 1) * own]
+        out_ref[k, own:] = both[cols + k * share:cols + (k + 1) * share]
 
 
 def inner_products(blended, projected, count):

time: 111 us -> 111 us (level)
  no operation moved by 1% of the time
where the time goes in v8:
time: 111 us; the launch traced here: 110 us
  blocking collectives  90.4 us (81%)
  Pallas kernels  9.65 us (9%)
  waiting for transfers between devices  3.62 us (3%)
  starting transfers between devices  3.31 us (3%)
  other arithmetic  1.54 us (1%)
    all_to_all x1, blocking collectives, body(): lax.all_to_all(partial.reshape(lines), plane, 0, 0).reshape(rows, RANK)  33.1 us
    all_to_all x1, blocking collectives, body(): lax.all_to_all(copies.reshape(lines), plane, 0, 0).reshape(rows, RANK)  20.9 us
    all_to_all x2, blocking collectives, gather(): lax.all_to_all(jnp.broadcast_to(block, (count,) + block.shape), axes, 0, 0)  20.9 us
    all_to_all x1, blocking collectives, scatter_sum(): return jnp.sum(lax.all_to_all(blocks, axes, 0, 0), axis=0)  15.5 us
    pallas_call x1, Pallas kernels, whiten_right(): pl.pallas_call(whiten_kernel, out_shape=(jax.ShapeDtypeStruct((RANK, RANK...  4.64 us
    all_to_all x1, waiting for transfers between devices, body(): squares = lax.all_to_all(squares, 'tensor', 0, 0)  3.62 us
    all_to_all x1, starting transfers between devices, body(): squares = lax.all_to_all(squares, 'tensor', 0, 0)  3.31 us
    pallas_call x1, Pallas kernels, left_and_moment(): pl.pallas_call(moment_kernel, out_shape=(jax.ShapeDtypeStruct((rows, RANK...  2.75 us
  transfers between devices with their start and end apart: 1, of which 1 were waited for; matrix products, arithmetic and copies ran while one was open for 0% of the time, Pallas kernels for 2%

profile of v8, /device:TPU:1, one launch (start us, length us, event | category | flops | bytes accessed | tf_op | source)
XLA Modules:
  0.0 110.3 jit_solution(12534186853150203753)
XLA Ops:
  0.6 0.0 copy-start
  0.6 1.4 %add_bitcast_fusion.blended_ref = f32[896,256]{1,0:T(8,128)S(1)} fusion(f32[1,1,896,256]{3,2,1,0:T(8,128)} %param.3, bf16[1,1,896,256]{3,2,1,0:T(8,128)(2,1)} %param.4), kind=kLoop, calls=%fused_computation | loop fusion | flops 458752 | bytes 2293760 | tf_op jit(solution)/shard_map/add | solution.py:274
  2.1 0.0 copy-done
  2.1 0.9 fusion
  3.0 33.1 %all_to_all.30 = f32[64,1,1792]{2,1,0:T(1,128)S(1)} all-to-all(f32[64,1,1792]{2,1,0:T(1,128)S(1)} %bitcast.17), channel_id=1, replica_groups=mesh['dp_far'=4,'dp_near'=2,'fsdp'=8,'tensor'=8] {'dp_far','dp_near','te..., dimensions={0} | all-to-all | bytes 917504 | tf_op jit(solution)/shard_map/all_to_all | solution.py:280
  36.1 0.1 reduce_sum.27
  36.3 20.9 %all_to_all.31 = f32[64,1,1792]{2,1,0:T(1,128)S(1)} all-to-all(f32[64,1,1792]{2,1,0:T(1,128)S(1)} %bitcast.16), channel_id=1, replica_groups=mesh['dp_far'=4,'dp_near'=2,'fsdp'=8,'tensor'=8] {'dp_far','dp_near','te..., dimensions={0} | all-to-all | bytes 917504 | tf_op jit(solution)/shard_map/all_to_all | solution.py:283
  57.2 1.0 shard_map.58
  58.2 15.5 %all_to_all.32 = f32[16,24,128]{2,1,0:T(8,128)S(1)} all-to-all(f32[16,24,128]{2,1,0:T(8,128)S(1)} %shard_map.58), channel_id=1, replica_groups=mesh['dp_far'=4,'dp_near'=2,'fsdp'=8,'tensor'=8] {'fsdp','dp_near'}, dimensions={0} | all-to-all | bytes 393216 | tf_op jit(solution)/shard_map/all_to_all | solution.py:265
  73.7 9.6 %all_to_all.33 = f32[4,16,128]{2,1,0:T(8,128)S(1)} all-to-all(f32[4,16,128]{2,1,0:T(8,128)S(1)} %broadcast_in_dim.19), channel_id=1, replica_groups=mesh['dp_far'=4,'dp_near'=2,'fsdp'=8,'tensor'=8] {'dp_far'}, dimensions={0} | all-to-all | bytes 65536 | tf_op jit(solution)/shard_map/all_to_all | solution.py:269
  83.3 11.3 %all_to_all.34.whole_ref = f32[16,24,128]{2,1,0:T(8,128)S(1)} all-to-all(f32[16,24,128]{2,1,0:T(8,128)S(1)} %broadcast_in_dim.20), channel_id=1, replica_groups=mesh['dp_far'=4,'dp_near'=2,'fsdp'=8,'tensor'=8] {'fsdp','dp_near'}, dimensions={0} | all-to-all | bytes 393216 | tf_op jit(solution)/shard_map/all_to_all | solution.py:269
  94.6 4.6 %shard_map.59 = (f32[128,128]{1,0:T(8,128)S(1)}, f32[256,128]{1,0:T(8,128)S(1)}, f32[8,1,128]{2,1,0:T(1,128)}) custom-call(f32[16,24,128]{2,1,0:T(8,128)S(1)} %all_to_all.34.whole_ref), custom_call_target="tpu_custom_call" | custom-call | tf_op jit(solution)/shard_map/pallas_call | solution.py:134
  99.3 3.3 %all-to-all-start.5 = ((f32[8,1,128]{2,1,0:T(1,128)}), f32[8,1,128]{2,1,0:T(1,128)S(1)}, u32[]{:S(2)}, u32[]{:S(2)}) async-start(f32[8,1,128]{2,1,0:T(1,128)} %get-tuple-element.22), calls=%async_computation.5 | async-start | bytes 8192 | tf_op jit(solution)/shard_map/all_to_all | solution.py:292
  102.6 2.7 %shard_map.60 = (f32[896,128]{1,0:T(8,128)S(1)}, f32[896,256]{1,0:T(8,128)}) custom-call(f32[896,256]{1,0:T(8,128)S(1)} %add_bitcast_fusion.blended_ref, f32[896,128]{1,0:T(8,128)S(1)} %bitcast.14, f32[128,128]{1,0:T(8,128)S(1)} %get-tuple-element.18.inverse_ref, f32[256,128]{1,0:T(8,128)S(1)} %get-tuple-element.19.reduced_ref), custom_call_target="tpu_custom_call" | custom-call | flops 352321536 | bytes 917504 | tf_op jit(solution)/shard_map/pallas_call | solution.py:208
  105.4 3.6 %all-to-all-done.5.squares_ref = f32[8,1,128]{2,1,0:T(1,128)S(1)} async-done(((f32[8,1,128]{2,1,0:T(1,128)}), f32[8,1,128]{2,1,0:T(1,128)S(1)}, u32[]{:S(2)}, u32[]{:S(2)}) %all-to-all-start.5) | async-done | bytes 4128 | tf_op jit(solution)/shard_map/all_to_all | solution.py:292
  109.0 1.3 %shard_map.61 = (f32[256,128]{1,0:T(8,128)}, bf16[896,256]{1,0:T(8,128)(2,1)}) custom-call(f32[896,128]{1,0:T(8,128)S(1)} %get-tuple-element.21.left_ref, f32[256,128]{1,0:T(8,128)S(1)} %get-tuple-element.19.reduced_ref, f32[8,1,128]{2,1,0:T(1,128)S(1)} %all-to-all-done.5.squares_ref), custom_call_target="tpu_custom_call" | custom-call | tf_op jit(solution)/shard_map/pallas_call | solution.py:247
  (10 shorter events, 0.2 us)
Async XLA Ops:
  0.6 1.4 %copy-start = (f32[1,256,128]{2,1,0:T(8,128)S(1)}, f32[1,256,128]{2,1,0:T(8,128)}, u32[]{:S(2)}) copy-start(f32[1,256,128]{2,1,0:T(8,128)} %param.5) | copy-start | bytes 393220
  99.3 9.7 %all-to-all-start.5 = ((f32[8,1,128]{2,1,0:T(1,128)}), f32[8,1,128]{2,1,0:T(1,128)S(1)}, u32[]{:S(2)}, u32[]{:S(2)}) async-start(f32[8,1,128]{2,1,0:T(1,128)} %get-tuple-element.22), calls=%async_computation.5 | async-start | bytes 8192 | tf_op jit(solution)/shard_map/all_to_all | solution.py:292

commit v9 on v8

--- a/solution.py
+++ b/solution.py
@@ -19,16 +19,6 @@
 epsilon = 1e-06
 
 
-def product(left, right):
-    return jnp.dot(left, right, precision=highest, preferred_element_type=jnp.float32)
-
-
-def inner_rows(left, right):
-    return lax.dot_general(
-        left, right, (((0,), (0,)), ((), ())), precision=highest, preferred_element_type=jnp.float32
-    )
-
-
 def outer_cols(left, right):
     return lax.dot_general(
         left, right, (((1,), (1,)), ((), ())), precision=highest, preferred_element_type=jnp.float32
@@ -45,6 +35,15 @@
 
 def dot(left, right):
     return jnp.dot(left, right, preferred_element_type=jnp.float32)
+
+
+def six_products(left, right):
+    l1, l2, l3 = left
+    r1, r2, r3 = right
+    pair = jnp.concatenate([r1, r2], axis=1)
+    high, low = dot(l1, pair), dot(l2, pair)
+    rest = low[:, RANK:] + (dot(l1, r3) + dot(l3, r1))
+    return high[:, :RANK] + ((high[:, RANK:] + low[:, :RANK]) + rest)
 
 
 def spread(row):
@@ -144,17 +143,27 @@
     )(whole)
 
 
+def project_kernel(blended_ref, right_ref, out_ref):
+    out_ref[...] = six_products(terms(blended_ref[...]), terms(right_ref[...]))
+
+
+def project(blended, right):
+    vmem = pl.BlockSpec(memory_space=pltpu.VMEM)
+    return pl.pallas_call(
+        project_kernel,
+        out_shape=jax.ShapeDtypeStruct((blended.shape[0], RANK), jnp.float32),
+        in_specs=[vmem] * 2,
+        out_specs=vmem,
+        compiler_params=pltpu.CompilerParams(vmem_limit_bytes=24 * 2**20),
+    )(blended, right)
+
+
 def inner_kernel(blended_ref, projected_ref, out_ref):
     count, share = out_ref.shape[0], RANK // out_ref.shape[0]
     own = out_ref.shape[1] - share
     cols = count * own
     projected = projected_ref[...]
-    r1, r2, r3 = terms(projected)
-    l1, l2, l3 = terms(jnp.concatenate([blended_ref[...], projected], axis=1).T)
-    pair = jnp.concatenate([r1, r2], axis=1)
-    high, low = dot(l1, pair), dot(l2, pair)
-    rest = low[:, RANK:] + (dot(l1, r3) + dot(l3, r1))
-    both = high[:, :RANK] + ((high[:, RANK:] + low[:, :RANK]) + rest)
+    both = six_products(terms(jnp.concatenate([blended_ref[...], projected], axis=1).T), terms(projected))
     for k in range(count):
         out_ref[k, :own] = both[k * own:(k + 1) * own]
         out_ref[k, own:] = both[cols + k * share:cols + (k + 1) * share]
@@ -276,7 +285,7 @@
     plane = ("dp_far", "dp_near", "tensor")
     count = n_far * n_near * n_tensor
     blocks, lines = (count, rows // count, RANK), (count, 1, rows // count * RANK)
-    partial = lax.optimization_barrier(product(blended, right_factor[0]))
+    partial = lax.optimization_barrier(project(blended, right_factor[0]))
     parts = lax.all_to_all(partial.reshape(lines), plane, 0, 0).reshape(rows, RANK)
     part = jnp.sum(lax.optimization_barrier(parts).reshape(blocks), axis=0)
     copies = lax.optimization_barrier(jnp.broadcast_to(part, blocks).reshape(rows, RANK))

time: 111 us -> 110 us (level)
  no operation moved by 1% of the time
where the time goes in v9:
time: 110 us
  blocking collectives  90.4 us (82%)
  Pallas kernels  10.3 us (9%)
  waiting for transfers between devices  3.62 us (3%)
  starting transfers between devices  3.31 us (3%)
  other arithmetic  1.54 us (1%)
    all_to_all x1, blocking collectives, body(): lax.all_to_all(partial.reshape(lines), plane, 0, 0).reshape(rows, RANK)  33.1 us
    all_to_all x1, blocking collectives, body(): lax.all_to_all(copies.reshape(lines), plane, 0, 0).reshape(rows, RANK)  20.9 us
    all_to_all x2, blocking collectives, gather(): lax.all_to_all(jnp.broadcast_to(block, (count,) + block.shape), axes, 0, 0)  20.9 us
    all_to_all x1, blocking collectives, scatter_sum(): return jnp.sum(lax.all_to_all(blocks, axes, 0, 0), axis=0)  15.5 us
    pallas_call x1, Pallas kernels, whiten_right(): pl.pallas_call(whiten_kernel, out_shape=(jax.ShapeDtypeStruct((RANK, RANK...  4.64 us
    all_to_all x1, waiting for transfers between devices, body(): squares = lax.all_to_all(squares, 'tensor', 0, 0)  3.62 us
    all_to_all x1, starting transfers between devices, body(): squares = lax.all_to_all(squares, 'tensor', 0, 0)  3.31 us
    pallas_call x1, Pallas kernels, left_and_moment(): pl.pallas_call(moment_kernel, out_shape=(jax.ShapeDtypeStruct((rows, RANK...  2.75 us
  transfers between devices with their start and end apart: 1, of which 1 were waited for; matrix products, arithmetic and copies ran while one was open for 0% of the time, Pallas kernels for 2%

profile of v9, /device:TPU:1, one launch (start us, length us, event | category | flops | bytes accessed | tf_op | source)
XLA Modules:
  0.0 110.0 jit_solution(6255930134535216604)
XLA Ops:
  0.6 0.0 copy-start
  0.6 1.4 %add_bitcast_fusion.blended_ref = f32[896,256]{1,0:T(8,128)S(1)} fusion(f32[1,1,896,256]{3,2,1,0:T(8,128)} %param.3, bf16[1,1,896,256]{3,2,1,0:T(8,128)(2,1)} %param.4), kind=kLoop, calls=%fused_computation | loop fusion | flops 458752 | bytes 2293760 | tf_op jit(solution)/shard_map/add | solution.py:283
  2.1 0.0 copy-done
  2.1 0.7 shard_map.58
  2.7 33.1 %all_to_all.30 = f32[64,1,1792]{2,1,0:T(1,128)S(1)} all-to-all(f32[64,1,1792]{2,1,0:T(1,128)S(1)} %bitcast.12), channel_id=1, replica_groups=mesh['dp_far'=4,'dp_near'=2,'fsdp'=8,'tensor'=8] {'dp_far','dp_near','te..., dimensions={0} | all-to-all | bytes 917504 | tf_op jit(solution)/shard_map/all_to_all | solution.py:289
  35.9 0.1 reduce_sum.27
  36.0 20.9 %all_to_all.31 = f32[64,1,1792]{2,1,0:T(1,128)S(1)} all-to-all(f32[64,1,1792]{2,1,0:T(1,128)S(1)} %bitcast.15), channel_id=1, replica_groups=mesh['dp_far'=4,'dp_near'=2,'fsdp'=8,'tensor'=8] {'dp_far','dp_near','te..., dimensions={0} | all-to-all | bytes 917504 | tf_op jit(solution)/shard_map/all_to_all | solution.py:292
  56.9 1.0 shard_map.59
  57.9 15.5 %all_to_all.32 = f32[16,24,128]{2,1,0:T(8,128)S(1)} all-to-all(f32[16,24,128]{2,1,0:T(8,128)S(1)} %shard_map.59), channel_id=1, replica_groups=mesh['dp_far'=4,'dp_near'=2,'fsdp'=8,'tensor'=8] {'fsdp','dp_near'}, dimensions={0} | all-to-all | bytes 393216 | tf_op jit(solution)/shard_map/all_to_all | solution.py:274
  73.5 9.6 %all_to_all.33 = f32[4,16,128]{2,1,0:T(8,128)S(1)} all-to-all(f32[4,16,128]{2,1,0:T(8,128)S(1)} %broadcast_in_dim.19), channel_id=1, replica_groups=mesh['dp_far'=4,'dp_near'=2,'fsdp'=8,'tensor'=8] {'dp_far'}, dimensions={0} | all-to-all | bytes 65536 | tf_op jit(solution)/shard_map/all_to_all | solution.py:278
  83.1 11.3 %all_to_all.34.whole_ref = f32[16,24,128]{2,1,0:T(8,128)S(1)} all-to-all(f32[16,24,128]{2,1,0:T(8,128)S(1)} %broadcast_in_dim.20), channel_id=1, replica_groups=mesh['dp_far'=4,'dp_near'=2,'fsdp'=8,'tensor'=8] {'fsdp','dp_near'}, dimensions={0} | all-to-all | bytes 393216 | tf_op jit(solution)/shard_map/all_to_all | solution.py:278
  94.4 4.6 %shard_map.60 = (f32[128,128]{1,0:T(8,128)S(1)}, f32[256,128]{1,0:T(8,128)S(1)}, f32[8,1,128]{2,1,0:T(1,128)}) custom-call(f32[16,24,128]{2,1,0:T(8,128)S(1)} %all_to_all.34.whole_ref), custom_call_target="tpu_custom_call" | custom-call | tf_op jit(solution)/shard_map/pallas_call | solution.py:133
  99.0 3.3 %all-to-all-start.5 = ((f32[8,1,128]{2,1,0:T(1,128)}), f32[8,1,128]{2,1,0:T(1,128)S(1)}, u32[]{:S(2)}, u32[]{:S(2)}) async-start(f32[8,1,128]{2,1,0:T(1,128)} %get-tuple-element.22), calls=%async_computation.5 | async-start | bytes 8192 | tf_op jit(solution)/shard_map/all_to_all | solution.py:301
  102.4 2.7 %shard_map.61 = (f32[896,128]{1,0:T(8,128)S(1)}, f32[896,256]{1,0:T(8,128)}) custom-call(f32[896,256]{1,0:T(8,128)S(1)} %add_bitcast_fusion.blended_ref, f32[896,128]{1,0:T(8,128)S(1)} %bitcast.11, f32[128,128]{1,0:T(8,128)S(1)} %get-tuple-element.18.inverse_ref, f32[256,128]{1,0:T(8,128)S(1)} %get-tuple-element.19.reduced_ref), custom_call_target="tpu_custom_call" | custom-call | flops 352321536 | bytes 917504 | tf_op jit(solution)/shard_map/pallas_call | solution.py:217
  105.1 3.6 %all-to-all-done.5.squares_ref = f32[8,1,128]{2,1,0:T(1,128)S(1)} async-done(((f32[8,1,128]{2,1,0:T(1,128)}), f32[8,1,128]{2,1,0:T(1,128)S(1)}, u32[]{:S(2)}, u32[]{:S(2)}) %all-to-all-start.5) | async-done | bytes 4128 | tf_op jit(solution)/shard_map/all_to_all | solution.py:301
  108.7 1.3 %shard_map.62 = (f32[256,128]{1,0:T(8,128)}, bf16[896,256]{1,0:T(8,128)(2,1)}) custom-call(f32[896,128]{1,0:T(8,128)S(1)} %get-tuple-element.21.left_ref, f32[256,128]{1,0:T(8,128)S(1)} %get-tuple-element.19.reduced_ref, f32[8,1,128]{2,1,0:T(1,128)S(1)} %all-to-all-done.5.squares_ref), custom_call_target="tpu_custom_call" | custom-call | tf_op jit(solution)/shard_map/pallas_call | solution.py:256
  (10 shorter events, 0.2 us)
Async XLA Ops:
  0.6 1.4 %copy-start = (f32[1,256,128]{2,1,0:T(8,128)S(1)}, f32[1,256,128]{2,1,0:T(8,128)}, u32[]{:S(2)}) copy-start(f32[1,256,128]{2,1,0:T(8,128)} %param.5) | copy-start | bytes 393220
  99.0 9.7 %all-to-all-start.5 = ((f32[8,1,128]{2,1,0:T(1,128)}), f32[8,1,128]{2,1,0:T(1,128)S(1)}, u32[]{:S(2)}, u32[]{:S(2)}) async-start(f32[8,1,128]{2,1,0:T(1,128)} %get-tuple-element.22), calls=%async_computation.5 | async-start | bytes 8192 | tf_op jit(solution)/shard_map/all_to_all | solution.py:301

commit v10 on v9

--- a/solution.py
+++ b/solution.py
@@ -290,7 +290,7 @@
     part = jnp.sum(lax.optimization_barrier(parts).reshape(blocks), axis=0)
     copies = lax.optimization_barrier(jnp.broadcast_to(part, blocks).reshape(rows, RANK))
     projected = lax.all_to_all(copies.reshape(lines), plane, 0, 0).reshape(rows, RANK)
-    group = ("fsdp", "dp_near")
+    group = ("dp_near", "fsdp")
     count = n_fsdp * n_near
     own = cols // count
     held = scatter_sum(inner_products(blended, projected, count), group)

time: 110 us -> 110 us (level)
  no operation moved by 1% of the time
where the time goes in v10:
time: 110 us
  blocking collectives  90.4 us (82%)
  Pallas kernels  10.3 us (9%)
  waiting for transfers between devices  3.62 us (3%)
  starting transfers between devices  3.31 us (3%)
  other arithmetic  1.54 us (1%)
    all_to_all x1, blocking collectives, body(): lax.all_to_all(partial.reshape(lines), plane, 0, 0).reshape(rows, RANK)  33.1 us
    all_to_all x2, blocking collectives, gather(): lax.all_to_all(jnp.broadcast_to(block, (count,) + block.shape), axes, 0, 0)  20.9 us
    all_to_all x1, blocking collectives, body(): lax.all_to_all(copies.reshape(lines), plane, 0, 0).reshape(rows, RANK)  20.9 us
    all_to_all x1, blocking collectives, scatter_sum(): return jnp.sum(lax.all_to_all(blocks, axes, 0, 0), axis=0)  15.4 us
    pallas_call x1, Pallas kernels, whiten_right(): pl.pallas_call(whiten_kernel, out_shape=(jax.ShapeDtypeStruct((RANK, RANK...  4.64 us
    all_to_all x1, waiting for transfers between devices, body(): squares = lax.all_to_all(squares, 'tensor', 0, 0)  3.62 us
    all_to_all x1, starting transfers between devices, body(): squares = lax.all_to_all(squares, 'tensor', 0, 0)  3.31 us
    pallas_call x1, Pallas kernels, left_and_moment(): pl.pallas_call(moment_kernel, out_shape=(jax.ShapeDtypeStruct((rows, RANK...  2.75 us
  transfers between devices with their start and end apart: 1, of which 1 were waited for; matrix products, arithmetic and copies ran while one was open for 0% of the time, Pallas kernels for 2%

profile of v10, /device:TPU:1, one launch (start us, length us, event | category | flops | bytes accessed | tf_op | source)
XLA Modules:
  0.0 110.0 jit_solution(6036506509841012216)
XLA Ops:
  0.6 0.0 copy-start
  0.6 1.4 %add_bitcast_fusion.blended_ref = f32[896,256]{1,0:T(8,128)S(1)} fusion(f32[1,1,896,256]{3,2,1,0:T(8,128)} %param.3, bf16[1,1,896,256]{3,2,1,0:T(8,128)(2,1)} %param.4), kind=kLoop, calls=%fused_computation | loop fusion | flops 458752 | bytes 2293760 | tf_op jit(solution)/shard_map/add | solution.py:283
  2.1 0.0 copy-done
  2.1 0.7 shard_map.58
  2.7 33.1 %all_to_all.30 = f32[64,1,1792]{2,1,0:T(1,128)S(1)} all-to-all(f32[64,1,1792]{2,1,0:T(1,128)S(1)} %bitcast.12), channel_id=1, replica_groups=mesh['dp_far'=4,'dp_near'=2,'fsdp'=8,'tensor'=8] {'dp_far','dp_near','te..., dimensions={0} | all-to-all | bytes 917504 | tf_op jit(solution)/shard_map/all_to_all | solution.py:289
  35.9 0.1 reduce_sum.27
  36.0 20.9 %all_to_all.31 = f32[64,1,1792]{2,1,0:T(1,128)S(1)} all-to-all(f32[64,1,1792]{2,1,0:T(1,128)S(1)} %bitcast.15), channel_id=1, replica_groups=mesh['dp_far'=4,'dp_near'=2,'fsdp'=8,'tensor'=8] {'dp_far','dp_near','te..., dimensions={0} | all-to-all | bytes 917504 | tf_op jit(solution)/shard_map/all_to_all | solution.py:292
  56.9 1.0 shard_map.59
  57.9 15.4 %all_to_all.32 = f32[16,24,128]{2,1,0:T(8,128)S(1)} all-to-all(f32[16,24,128]{2,1,0:T(8,128)S(1)} %shard_map.59), channel_id=1, replica_groups=mesh['dp_far'=4,'dp_near'=2,'fsdp'=8,'tensor'=8] {'dp_near','fsdp'}, dimensions={0} | all-to-all | bytes 393216 | tf_op jit(solution)/shard_map/all_to_all | solution.py:274
  73.4 9.6 %all_to_all.33 = f32[4,16,128]{2,1,0:T(8,128)S(1)} all-to-all(f32[4,16,128]{2,1,0:T(8,128)S(1)} %broadcast_in_dim.19), channel_id=1, replica_groups=mesh['dp_far'=4,'dp_near'=2,'fsdp'=8,'tensor'=8] {'dp_far'}, dimensions={0} | all-to-all | bytes 65536 | tf_op jit(solution)/shard_map/all_to_all | solution.py:278
  83.0 11.4 %all_to_all.34.whole_ref = f32[16,24,128]{2,1,0:T(8,128)S(1)} all-to-all(f32[16,24,128]{2,1,0:T(8,128)S(1)} %broadcast_in_dim.20), channel_id=1, replica_groups=mesh['dp_far'=4,'dp_near'=2,'fsdp'=8,'tensor'=8] {'dp_near','fsdp'}, dimensions={0} | all-to-all | bytes 393216 | tf_op jit(solution)/shard_map/all_to_all | solution.py:278
  94.4 4.6 %shard_map.60 = (f32[128,128]{1,0:T(8,128)S(1)}, f32[256,128]{1,0:T(8,128)S(1)}, f32[8,1,128]{2,1,0:T(1,128)}) custom-call(f32[16,24,128]{2,1,0:T(8,128)S(1)} %all_to_all.34.whole_ref), custom_call_target="tpu_custom_call" | custom-call | tf_op jit(solution)/shard_map/pallas_call | solution.py:133
  99.0 3.3 %all-to-all-start.5 = ((f32[8,1,128]{2,1,0:T(1,128)}), f32[8,1,128]{2,1,0:T(1,128)S(1)}, u32[]{:S(2)}, u32[]{:S(2)}) async-start(f32[8,1,128]{2,1,0:T(1,128)} %get-tuple-element.22), calls=%async_computation.5 | async-start | bytes 8192 | tf_op jit(solution)/shard_map/all_to_all | solution.py:301
  102.4 2.7 %shard_map.61 = (f32[896,128]{1,0:T(8,128)S(1)}, f32[896,256]{1,0:T(8,128)}) custom-call(f32[896,256]{1,0:T(8,128)S(1)} %add_bitcast_fusion.blended_ref, f32[896,128]{1,0:T(8,128)S(1)} %bitcast.11, f32[128,128]{1,0:T(8,128)S(1)} %get-tuple-element.18.inverse_ref, f32[256,128]{1,0:T(8,128)S(1)} %get-tuple-element.19.reduced_ref), custom_call_target="tpu_custom_call" | custom-call | flops 352321536 | bytes 917504 | tf_op jit(solution)/shard_map/pallas_call | solution.py:217
  105.1 3.6 %all-to-all-done.5.squares_ref = f32[8,1,128]{2,1,0:T(1,128)S(1)} async-done(((f32[8,1,128]{2,1,0:T(1,128)}), f32[8,1,128]{2,1,0:T(1,128)S(1)}, u32[]{:S(2)}, u32[]{:S(2)}) %all-to-all-start.5) | async-done | bytes 4128 | tf_op jit(solution)/shard_map/all_to_all | solution.py:301
  108.7 1.3 %shard_map.62 = (f32[256,128]{1,0:T(8,128)}, bf16[896,256]{1,0:T(8,128)(2,1)}) custom-call(f32[896,128]{1,0:T(8,128)S(1)} %get-tuple-element.21.left_ref, f32[256,128]{1,0:T(8,128)S(1)} %get-tuple-element.19.reduced_ref, f32[8,1,128]{2,1,0:T(1,128)S(1)} %all-to-all-done.5.squares_ref), custom_call_target="tpu_custom_call" | custom-call | tf_op jit(solution)/shard_map/pallas_call | solution.py:256
  (10 shorter events, 0.2 us)
Async XLA Ops:
  0.6 1.4 %copy-start = (f32[1,256,128]{2,1,0:T(8,128)S(1)}, f32[1,256,128]{2,1,0:T(8,128)}, u32[]{:S(2)}) copy-start(f32[1,256,128]{2,1,0:T(8,128)} %param.5) | copy-start | bytes 393220
  99.0 9.7 %all-to-all-start.5 = ((f32[8,1,128]{2,1,0:T(1,128)}), f32[8,1,128]{2,1,0:T(1,128)S(1)}, u32[]{:S(2)}, u32[]{:S(2)}) async-start(f32[8,1,128]{2,1,0:T(1,128)} %get-tuple-element.22), calls=%async_computation.5 | async-start | bytes 8192 | tf_op jit(solution)/shard_map/all_to_all | solution.py:301

commit v11 on v9

--- a/solution.py
+++ b/solution.py
@@ -1,3 +1,4 @@
+import functools
 import math
 
 import jax
@@ -158,6 +159,27 @@
     )(blended, right)
 
 
+def resum_kernel(high, parts_ref, out_ref):
+    slab = high * SUB
+    starts = range(0, parts_ref.shape[0], slab)
+    total = sum(parts_ref[start:start + slab, :] for start in starts)
+    block = sum(total[k * high:(k + 1) * high] for k in range(SUB))
+    copies = jnp.concatenate([block] * SUB, axis=0)
+    for start in starts:
+        out_ref[start:start + slab, :] = copies
+
+
+def resum(parts, count):
+    vmem = pl.BlockSpec(memory_space=pltpu.VMEM)
+    return pl.pallas_call(
+        functools.partial(resum_kernel, parts.shape[0] // count),
+        out_shape=jax.ShapeDtypeStruct(parts.shape, jnp.float32),
+        in_specs=[vmem],
+        out_specs=vmem,
+        compiler_params=pltpu.CompilerParams(vmem_limit_bytes=16 * 2**20),
+    )(parts)
+
+
 def inner_kernel(blended_ref, projected_ref, out_ref):
     count, share = out_ref.shape[0], RANK // out_ref.shape[0]
     own = out_ref.shape[1] - share
@@ -284,11 +306,10 @@
     rows, cols = blended.shape
     plane = ("dp_far", "dp_near", "tensor")
     count = n_far * n_near * n_tensor
-    blocks, lines = (count, rows // count, RANK), (count, 1, rows // count * RANK)
+    lines = (count, 1, rows // count * RANK)
     partial = lax.optimization_barrier(project(blended, right_factor[0]))
     parts = lax.all_to_all(partial.reshape(lines), plane, 0, 0).reshape(rows, RANK)
-    part = jnp.sum(lax.optimization_barrier(parts).reshape(blocks), axis=0)
-    copies = lax.optimization_barrier(jnp.broadcast_to(part, blocks).reshape(rows, RANK))
+    copies = resum(parts, count)
     projected = lax.all_to_all(copies.reshape(lines), plane, 0, 0).reshape(rows, RANK)
     group = ("fsdp", "dp_near")
     count = n_fsdp * n_near

time: 110 us -> 110 us (level)
  no operation moved by 1% of the time
where the time goes in v11:
time: 110 us
  blocking collectives  90.4 us (82%)
  Pallas kernels  10.4 us (9%)
  waiting for transfers between devices  3.62 us (3%)
  starting transfers between devices  3.31 us (3%)
  other arithmetic  1.46 us (1%)
    all_to_all x1, blocking collectives, body(): lax.all_to_all(partial.reshape(lines), plane, 0, 0).reshape(rows, RANK)  33.1 us
    all_to_all x1, blocking collectives, body(): lax.all_to_all(copies.reshape(lines), plane, 0, 0).reshape(rows, RANK)  20.9 us
    all_to_all x2, blocking collectives, gather(): lax.all_to_all(jnp.broadcast_to(block, (count,) + block.shape), axes, 0, 0)  20.9 us
    all_to_all x1, blocking collectives, scatter_sum(): return jnp.sum(lax.all_to_all(blocks, axes, 0, 0), axis=0)  15.5 us
    pallas_call x1, Pallas kernels, whiten_right(): pl.pallas_call(whiten_kernel, out_shape=(jax.ShapeDtypeStruct((RANK, RANK...  4.64 us
    all_to_all x1, waiting for transfers between devices, body(): squares = lax.all_to_all(squares, 'tensor', 0, 0)  3.62 us
    all_to_all x1, starting transfers between devices, body(): squares = lax.all_to_all(squares, 'tensor', 0, 0)  3.31 us
    pallas_call x1, Pallas kernels, left_and_moment(): pl.pallas_call(moment_kernel, out_shape=(jax.ShapeDtypeStruct((rows, RANK...  2.75 us
  transfers between devices with their start and end apart: 1, of which 1 were waited for; matrix products, arithmetic and copies ran while one was open for 0% of the time, Pallas kernels for 2%

profile of v11, /device:TPU:1, one launch (start us, length us, event | category | flops | bytes accessed | tf_op | source)
XLA Modules:
  0.0 109.9 jit_solution(13931036636372269455)
XLA Ops:
  0.6 0.0 copy-start
  0.6 1.4 %add_bitcast_fusion.blended_ref = f32[896,256]{1,0:T(8,128)S(1)} fusion(f32[1,1,896,256]{3,2,1,0:T(8,128)} %param.3, bf16[1,1,896,256]{3,2,1,0:T(8,128)(2,1)} %param.4), kind=kLoop, calls=%fused_computation | loop fusion | flops 458752 | bytes 2293760 | tf_op jit(solution)/shard_map/add | solution.py:305
  2.1 0.0 copy-done
  2.1 0.7 shard_map.58
  2.7 33.1 %all_to_all.30 = f32[64,1,1792]{2,1,0:T(1,128)S(1)} all-to-all(f32[64,1,1792]{2,1,0:T(1,128)S(1)} %bitcast.14), channel_id=1, replica_groups=mesh['dp_far'=4,'dp_near'=2,'fsdp'=8,'tensor'=8] {'dp_far','dp_near','te..., dimensions={0} | all-to-all | bytes 917504 | tf_op jit(solution)/shard_map/all_to_all | solution.py:311
  35.8 0.1 shard_map.59
  35.9 20.9 %all_to_all.31 = f32[64,1,1792]{2,1,0:T(1,128)S(1)} all-to-all(f32[64,1,1792]{2,1,0:T(1,128)S(1)} %bitcast.13), channel_id=1, replica_groups=mesh['dp_far'=4,'dp_near'=2,'fsdp'=8,'tensor'=8] {'dp_far','dp_near','te..., dimensions={0} | all-to-all | bytes 917504 | tf_op jit(solution)/shard_map/all_to_all | solution.py:313
  56.8 1.0 shard_map.60
  57.8 15.5 %all_to_all.32 = f32[16,24,128]{2,1,0:T(8,128)S(1)} all-to-all(f32[16,24,128]{2,1,0:T(8,128)S(1)} %shard_map.60), channel_id=1, replica_groups=mesh['dp_far'=4,'dp_near'=2,'fsdp'=8,'tensor'=8] {'fsdp','dp_near'}, dimensions={0} | all-to-all | bytes 393216 | tf_op jit(solution)/shard_map/all_to_all | solution.py:296
  73.4 9.6 %all_to_all.33 = f32[4,16,128]{2,1,0:T(8,128)S(1)} all-to-all(f32[4,16,128]{2,1,0:T(8,128)S(1)} %broadcast_in_dim.15), channel_id=1, replica_groups=mesh['dp_far'=4,'dp_near'=2,'fsdp'=8,'tensor'=8] {'dp_far'}, dimensions={0} | all-to-all | bytes 65536 | tf_op jit(solution)/shard_map/all_to_all | solution.py:300
  83.0 11.3 %all_to_all.34.whole_ref = f32[16,24,128]{2,1,0:T(8,128)S(1)} all-to-all(f32[16,24,128]{2,1,0:T(8,128)S(1)} %broadcast_in_dim.16), channel_id=1, replica_groups=mesh['dp_far'=4,'dp_near'=2,'fsdp'=8,'tensor'=8] {'fsdp','dp_near'}, dimensions={0} | all-to-all | bytes 393216 | tf_op jit(solution)/shard_map/all_to_all | solution.py:300
  94.2 4.6 %shard_map.61 = (f32[128,128]{1,0:T(8,128)S(1)}, f32[256,128]{1,0:T(8,128)S(1)}, f32[8,1,128]{2,1,0:T(1,128)}) custom-call(f32[16,24,128]{2,1,0:T(8,128)S(1)} %all_to_all.34.whole_ref), custom_call_target="tpu_custom_call" | custom-call | tf_op jit(solution)/shard_map/pallas_call | solution.py:134
  98.9 3.3 %all-to-all-start.5 = ((f32[8,1,128]{2,1,0:T(1,128)}), f32[8,1,128]{2,1,0:T(1,128)S(1)}, u32[]{:S(2)}, u32[]{:S(2)}) async-start(f32[8,1,128]{2,1,0:T(1,128)} %get-tuple-element.22), calls=%async_computation.5 | async-start | bytes 8192 | tf_op jit(solution)/shard_map/all_to_all | solution.py:322
  102.2 2.7 %shard_map.62 = (f32[896,128]{1,0:T(8,128)S(1)}, f32[896,256]{1,0:T(8,128)}) custom-call(f32[896,256]{1,0:T(8,128)S(1)} %add_bitcast_fusion.blended_ref, f32[896,128]{1,0:T(8,128)S(1)} %bitcast.11, f32[128,128]{1,0:T(8,128)S(1)} %get-tuple-element.18.inverse_ref, f32[256,128]{1,0:T(8,128)S(1)} %get-tuple-element.19.reduced_ref), custom_call_target="tpu_custom_call" | custom-call | flops 352321536 | bytes 917504 | tf_op jit(solution)/shard_map/pallas_call | solution.py:239
  105.0 3.6 %all-to-all-done.5.squares_ref = f32[8,1,128]{2,1,0:T(1,128)S(1)} async-done(((f32[8,1,128]{2,1,0:T(1,128)}), f32[8,1,128]{2,1,0:T(1,128)S(1)}, u32[]{:S(2)}, u32[]{:S(2)}) %all-to-all-start.5) | async-done | bytes 4128 | tf_op jit(solution)/shard_map/all_to_all | solution.py:322
  108.6 1.3 %shard_map.63 = (f32[256,128]{1,0:T(8,128)}, bf16[896,256]{1,0:T(8,128)(2,1)}) custom-call(f32[896,128]{1,0:T(8,128)S(1)} %get-tuple-element.21.left_ref, f32[256,128]{1,0:T(8,128)S(1)} %get-tuple-element.19.reduced_ref, f32[8,1,128]{2,1,0:T(1,128)S(1)} %all-to-all-done.5.squares_ref), custom_call_target="tpu_custom_call" | custom-call | tf_op jit(solution)/shard_map/pallas_call | solution.py:278
  (7 shorter events, 0.1 us)
Async XLA Ops:
  0.6 1.4 %copy-start = (f32[1,256,128]{2,1,0:T(8,128)S(1)}, f32[1,256,128]{2,1,0:T(8,128)}, u32[]{:S(2)}) copy-start(f32[1,256,128]{2,1,0:T(8,128)} %param.5) | copy-start | bytes 393220
  98.9 9.7 %all-to-all-start.5 = ((f32[8,1,128]{2,1,0:T(1,128)}), f32[8,1,128]{2,1,0:T(1,128)S(1)}, u32[]{:S(2)}, u32[]{:S(2)}) async-start(f32[8,1,128]{2,1,0:T(1,128)} %get-tuple-element.22), calls=%async_computation.5 | async-start | bytes 8192 | tf_op jit(solution)/shard_map/all_to_all | solution.py:322
